TPU v7x, 256 devices: a whole 4x4x8 slice. The times are simulated.
256 devices in a mesh: pipe: 16 (over x, y_lo, core), expert: 16 (over z, y_hi).
Axes of the slice: x: 4, y: 4 (y_hi: 2, y_lo: 2; y = y_hi * 2 + y_lo), z: 8, core: 2. Of those that a mesh axis runs over, the one named last changes fastest.
Arguments:
- fwd_rows: bfloat16 [16, 1024, 3584], P('pipe', 'expert'), may hold values from -3 to 3
- fwd_experts: int32 [16, 1024, 2], P('pipe', 'expert'), may hold values from 0 to 3, as said below
- fwd_weight: bfloat16 [16, 1024, 2], P('pipe', 'expert'), may hold values from 0.5 to 1.5
- back_rows: bfloat16 [16, 1024, 3584], P('pipe', 'expert'), may hold values from -3 to 3
- back_experts: int32 [16, 1024, 2], P('pipe', 'expert'), may hold values from 0 to 3, as said below
- back_weight: bfloat16 [16, 1024, 2], P('pipe', 'expert'), may hold values from 0.5 to 1.5
- back_cotangent: bfloat16 [16, 1024, 3584], P('pipe', 'expert'), may hold values from -6 to 6
- norm_gain: bfloat16 [16, 3584], P('pipe'), may hold values from 0.099609375 to 1.8984375
- w_gate: bfloat16 [16, 16, 3584, 256], P('pipe', 'expert'), may hold values from -0.09375 to 0.09375
- w_up: bfloat16 [16, 16, 3584, 256], P('pipe', 'expert'), may hold values from -0.09375 to 0.09375
- w_down: bfloat16 [16, 16, 256, 3584], P('pipe', 'expert'), may hold values from -0.1875 to 0.1875
- saved_gate: bfloat16 [16, 16, 512, 256], P('pipe', 'expert'), may hold values from -6 to 6
- saved_up: bfloat16 [16, 16, 512, 256], P('pipe', 'expert'), may hold values from -6 to 6
Outputs:
- next_input: bfloat16 [16, 1024, 3584], P('pipe', 'expert')
- prev_grad: bfloat16 [16, 1024, 3584], P('pipe', 'expert')
Inputs may be any that keep to these rules, and one draw needn't show every extreme that they name: `fwd_experts`: each token names 2 different experts; in every aligned block of 64 tokens each expert is named exactly 32 times. `back_experts`: each token names 2 different experts; in every aligned block of 64 tokens each expert is named exactly 32 times.
All inputs are finite; a program needn't handle non-finite values.
Results may differ from a plain program's by a relative error of at most 0.0065.
Values may be sent and summed in bfloat16 or wider, within the bound.
A program may use at most 64 MiB of HBM per device.

v0:
```python
import jax
import jax.numpy as jnp
from jax import lax
from jax.sharding import PartitionSpec as P

EXPERTS = 4
CAP = 32


epsilon = 1e-06


def from_behind(value, axis, steps):
    count = lax.axis_size(axis)
    leading, last = (max(0, -steps), min(count, count - steps))
    return lax.ppermute(value, axis, [(source, source + steps) for source in range(leading, last)])


def normalize(rows_in, gain_wide):
    widened = rows_in.astype(jnp.float32)
    rscale = lax.rsqrt(jnp.mean(widened * widened, axis=-1, keepdims=True) + epsilon)
    unit_rows = widened * rscale
    return ((unit_rows * gain_wide).astype(jnp.bfloat16), unit_rows, rscale)


def transposed(left, right):
    return lax.dot_general(
        left, right, (((1,), (1,)), ((), ())), preferred_element_type=jnp.float32
    )


def route_tables(expert_ids):
    token_count = expert_ids.shape[0]
    one_hot = (
        expert_ids[:, :, None] == jnp.arange(EXPERTS, dtype=jnp.int32)[None, None, :]
    ).astype(jnp.int32)
    named = jnp.sum(one_hot, axis=1, dtype=jnp.int32)
    ranks = jnp.cumsum(named, axis=0, dtype=jnp.int32) - named
    slot_of = jnp.sum(one_hot * ranks[:, None, :], axis=2, dtype=jnp.int32)
    positions = jnp.broadcast_to(
        jnp.arange(token_count, dtype=jnp.int32)[:, None], expert_ids.shape
    )
    token_of = jnp.zeros((EXPERTS, CAP), jnp.int32).at[expert_ids, slot_of].set(positions)
    return (one_hot, slot_of, token_of)


def combine_rows(returned, expert_ids, slot_of, split_count):
    width = returned.shape[-1]
    summed = jnp.sum(returned.reshape(EXPERTS, split_count, CAP, width), axis=1, dtype=jnp.float32)
    flat_rows = summed.reshape(EXPERTS * CAP, width)
    return jnp.take(flat_rows, expert_ids * CAP + slot_of, axis=0)


def body(
    fwd_rows,
    fwd_experts,
    fwd_weight,
    back_rows,
    back_experts,
    back_weight,
    back_cotangent,
    norm_gain,
    w_gate,
    w_up,
    w_down,
    saved_gate,
    saved_up,
):
    shard_count = lax.axis_size("expert")
    split_count = shard_count // EXPERTS
    gain_wide = norm_gain[0].astype(jnp.float32)
    fwd_local = fwd_rows[0]
    back_local = back_rows[0]
    cot_local = back_cotangent[0]
    gate_mat = w_gate[0, 0]
    up_mat = w_up[0, 0]
    down_mat = w_down[0, 0]
    gate_saved = saved_gate[0, 0]
    up_saved = saved_up[0, 0]
    width = fwd_local.shape[-1]
    fwd_ids = fwd_experts[0]
    back_ids = back_experts[0]
    fwd_hot, fwd_slot, fwd_token = route_tables(fwd_ids)
    back_hot, back_slot, back_token = route_tables(back_ids)
    weight_table = jnp.sum(
        back_weight[0].astype(jnp.float32)[:, :, None] * back_hot.astype(jnp.float32), axis=1
    )
    slot_weight = weight_table[back_token, jnp.arange(EXPERTS, dtype=jnp.int32)[:, None]].astype(
        jnp.bfloat16
    )
    weight_out = jnp.repeat(slot_weight, split_count, axis=0)
    source_rows = normalize(fwd_local, gain_wide)[0]
    outgoing_fwd = jnp.take(source_rows, jnp.repeat(fwd_token, split_count, axis=0), axis=0)
    outgoing_cot = jnp.take(cot_local, jnp.repeat(back_token, split_count, axis=0), axis=0)
    arrived = lax.all_to_all(outgoing_fwd, "expert", split_axis=0, concat_axis=0, tiled=True)
    flat_rows = arrived.reshape(-1, width)
    gate_f = jnp.dot(flat_rows, gate_mat, preferred_element_type=jnp.float32)
    up_f = jnp.dot(flat_rows, up_mat, preferred_element_type=jnp.float32)
    hidden_f = (jax.nn.silu(gate_f) * up_f).astype(jnp.bfloat16)
    partial_value = jnp.dot(hidden_f, down_mat, preferred_element_type=jnp.float32).astype(
        jnp.bfloat16
    )
    returned_fwd = lax.all_to_all(
        partial_value.reshape(arrived.shape[0], arrived.shape[1], width),
        "expert",
        split_axis=0,
        concat_axis=0,
        tiled=True,
    )
    cot_arrived, weight_arrived = (
        lax.all_to_all(outgoing_cot, "expert", split_axis=0, concat_axis=0, tiled=True),
        lax.all_to_all(weight_out, "expert", split_axis=0, concat_axis=0, tiled=True),
    )
    cot_flat = cot_arrived.reshape(-1, width)
    weight_flat = weight_arrived.reshape(-1).astype(jnp.float32)
    d_hidden = weight_flat[:, None] * transposed(cot_flat, down_mat)
    gate_b = gate_saved.astype(jnp.float32)
    up_b = up_saved.astype(jnp.float32)
    sigmoid_gate = jax.nn.sigmoid(gate_b)
    d_gate = (d_hidden * up_b * sigmoid_gate * (1.0 + gate_b * (1.0 - sigmoid_gate))).astype(
        jnp.bfloat16
    )
    d_up = (d_hidden * gate_b * sigmoid_gate).astype(jnp.bfloat16)
    partial_value = (transposed(d_gate, gate_mat) + transposed(d_up, up_mat)).astype(jnp.bfloat16)
    returned_back = lax.all_to_all(
        partial_value.reshape(cot_arrived.shape[0], cot_arrived.shape[1], width),
        "expert",
        split_axis=0,
        concat_axis=0,
        tiled=True,
    )
    picked_fwd = combine_rows(returned_fwd, fwd_ids, fwd_slot, split_count)
    branch = jnp.sum(fwd_weight[0].astype(jnp.float32)[:, :, None] * picked_fwd, axis=1)
    layer_out = (fwd_local.astype(jnp.float32) + branch).astype(jnp.bfloat16)
    next_input = from_behind(layer_out[None], "pipe", 1)
    d_normed = jnp.sum(combine_rows(returned_back, back_ids, back_slot, split_count), axis=1)
    unit_b, scale_b = normalize(back_local, gain_wide)[1:]
    d_unit = d_normed * gain_wide
    d_rows = scale_b * (d_unit - unit_b * jnp.mean(d_unit * unit_b, axis=-1, keepdims=True))
    grad_in = (cot_local.astype(jnp.float32) + d_rows).astype(jnp.bfloat16)
    prev_grad = from_behind(grad_in[None], "pipe", -1)
    return (next_input, prev_grad)


def solution(mesh):
    placed = (
        P("pipe", "expert", None),
        P("pipe", "expert", None),
        P("pipe", "expert", None),
        P("pipe", "expert", None),
        P("pipe", "expert", None),
        P("pipe", "expert", None),
        P("pipe", "expert", None),
        P("pipe", None),
        P("pipe", "expert", None, None),
        P("pipe", "expert", None, None),
        P("pipe", "expert", None, None),
        P("pipe", "expert", None, None),
        P("pipe", "expert", None, None),
    )
    return jax.shard_map(
        body,
        mesh=mesh,
        in_specs=placed,
        out_specs=(P("pipe", "expert", None), P("pipe", "expert", None)),
        check_vma=False,
    )
```

profile of v0, /device:TPU:37, one launch (start us, length us, event | category | flops | bytes accessed | tf_op | source)
XLA Modules:
  0.0 465.0 jit_solution(13182035801742223809)
XLA Ops:
  3.6 6.4 %scatter_fusion.1 = s32[4,32]{1,0:T(4,128)S(1)} fusion(s32[4,32]{1,0:T(4,128)S(1)} %broadcast.151.clone, s32[128]{0:T(128)S(1)} %reshape.318, s32[128]{0:T(128)S(1)} %reshape.314), kind=kCustom, calls=%fused_computation.6 | custom fusion | bytes 2560 | tf_op jit(solution)/shard_map/scatter | solution.py:43
  12.3 10.7 %all-to-all-start.2 = ((bf16[16,1,32]{2,1,0:T(2,128)(2,1)}), bf16[16,1,32]{2,1,0:T(2,128)(2,1)S(1)}, u32[]{:S(2)}, u32[]{:S(2)}) async-start(bf16[16,1,32]{2,1,0:T(2,128)(2,1)} %copy.83), calls=%async_computation.2 | async-start | bytes 16384 | tf_op jit(solution)/shard_map/all_to_all | solution.py:112
  23.1 4.2 gather_fusion.3
  27.3 4.2 broadcast_select_fusion
  31.6 9.1 %all-to-all-start.3 = ((bf16[16,32,3584]{2,1,0:T(8,128)(2,1)}), bf16[16,32,3584]{2,1,0:T(8,128)(2,1)}, u32[]{:S(2)}, u32[]{:S(2)}) async-start(bf16[16,32,3584]{2,1,0:T(8,128)(2,1)} %broadcast_select_fusion), calls=%async_computation.3 | async-start | bytes 7340032 | tf_op jit(solution)/shard_map/all_to_all | solution.py:111
  40.7 81.5 %all-to-all-done.3 = bf16[16,32,3584]{2,1,0:T(8,128)(2,1)} async-done(((bf16[16,32,3584]{2,1,0:T(8,128)(2,1)}), bf16[16,32,3584]{2,1,0:T(8,128)(2,1)}, u32[]{:S(2)}, u32[]{:S(2)}) %all-to-all-start.3) | async-done | bytes 3670048 | tf_op jit(solution)/shard_map/all_to_all | solution.py:111
  122.2 3.9 fusion.14
  130.5 8.8 %all-to-all-start.4 = ((bf16[16,32,3584]{2,1,0:T(8,128)(2,1)}), bf16[16,32,3584]{2,1,0:T(8,128)(2,1)}, u32[]{:S(2)}, u32[]{:S(2)}) async-start(bf16[16,32,3584]{2,1,0:T(8,128)(2,1)} %bitcast.125), calls=%async_computation.4 | async-start | bytes 7340032 | tf_op jit(solution)/shard_map/all_to_all | solution.py:125
  140.2 6.4 %scatter_fusion = s32[4,32]{1,0:T(4,128)S(1)} fusion(s32[4,32]{1,0:T(4,128)S(1)} %broadcast.151.clone.1, s32[128]{0:T(128)S(1)} %reshape.312, s32[128]{0:T(128)S(1)} %reshape.314), kind=kCustom, calls=%fused_computation.5 | custom fusion | bytes 2560 | tf_op jit(solution)/shard_map/scatter | solution.py:43
  148.2 72.3 %all-to-all-done.4 = bf16[16,32,3584]{2,1,0:T(8,128)(2,1)} async-done(((bf16[16,32,3584]{2,1,0:T(8,128)(2,1)}), bf16[16,32,3584]{2,1,0:T(8,128)(2,1)}, u32[]{:S(2)}, u32[]{:S(2)}) %all-to-all-start.4) | async-done | bytes 3670048 | tf_op jit(solution)/shard_map/all_to_all | solution.py:125
  220.5 4.1 convert_reduce_fusion
  224.6 4.7 %gather_fusion.4 = f32[128,3584]{1,0:T(8,128)} fusion(f32[128,3584]{1,0:T(8,128)} %bitcast.121, s32[1024]{0:T(1024)S(1)} %pad_clamp_fusion), kind=kCustom, calls=%fused_computation.3.clone | custom fusion | bytes 3670528 | tf_op jit(solution)/shard_map/jit(_take)/gather | solution.py:51
  232.5 4.4 select_reduce_fusion
  238.2 4.2 gather_fusion.1
  244.8 91.5 %all_to_all.29 = bf16[16,32,3584]{2,1,0:T(8,128)(2,1)S(1)} all-to-all(bf16[16,32,3584]{2,1,0:T(8,128)(2,1)S(1)} %broadcast_select_fusion.1), channel_id=1, replica_groups=mesh['pipe'=16,'expert'=16] {'expert'}, dimensions={0} | all-to-all | bytes 7340032 | tf_op jit(solution)/shard_map/all_to_all | solution.py:95
  339.2 8.4 %convolution_convert_fusion = bf16[512,3584]{1,0:T(8,128)(2,1)} fusion(bf16[1,1,256,3584]{3,2,1,0:T(8,128)(2,1)} %param.27, bf16[512,3584]{1,0:T(8,128)(2,1)} %bitcast.128, bf16[1,1,3584,256]{3,2,1,0:T(8,128)(2,1)S(1)} %copy-done, f32[512,256]{1,0:T(8,128)S(1)} %fusion.8), kind=kOutput, calls=%fused_computation.10 | convolution fusion | flops 1881669632 | bytes 11534336 | tf_op jit(solution)/shard_map/dot_general | solution.py:100
  347.6 6.8 %all-to-all-start.1 = ((bf16[16,32,3584]{2,1,0:T(8,128)(2,1)}), bf16[16,32,3584]{2,1,0:T(8,128)(2,1)}, u32[]{:S(2)}, u32[]{:S(2)}) async-start(bf16[16,32,3584]{2,1,0:T(8,128)(2,1)} %bitcast.126), calls=%async_computation.1 | async-start | bytes 7340032 | tf_op jit(solution)/shard_map/all_to_all | solution.py:103
  356.9 4.4 collective-permute-start.1
  361.3 74.2 %all-to-all-done.1 = bf16[16,32,3584]{2,1,0:T(8,128)(2,1)} async-done(((bf16[16,32,3584]{2,1,0:T(8,128)(2,1)}), bf16[16,32,3584]{2,1,0:T(8,128)(2,1)}, u32[]{:S(2)}, u32[]{:S(2)}) %all-to-all-start.1) | async-done | bytes 3670048 | tf_op jit(solution)/shard_map/all_to_all | solution.py:103
  435.6 4.1 convert_reduce_fusion.1
  439.6 4.7 %gather_fusion.2 = f32[128,3584]{1,0:T(8,128)} fusion(f32[128,3584]{1,0:T(8,128)} %bitcast.122, s32[1024]{0:T(1024)S(1)} %pad_clamp_fusion.2), kind=kCustom, calls=%fused_computation.1.clone | custom fusion | bytes 3670528 | tf_op jit(solution)/shard_map/jit(_take)/gather | solution.py:51
  447.6 4.7 %fusion.10 = f32[64,3584]{1,0:T(8,128)S(1)} fusion(f32[64,2,3584]{2,1,0:T(2,128)} %reshape.345, pred[64,2]{1,0:T(8,128)(4,1)S(1)} %copy.75, f32[64,2]{1,0:T(8,128)S(1)} %copy.71), kind=kLoop, calls=%fused_computation.25 | loop fusion | flops 1146880 | bytes 2753152 | tf_op jit(solution)/shard_map/reduce_sum | solution.py:133
  452.5 5.6 %collective-permute-start = (bf16[1,64,3584]{2,1,0:T(8,128)(2,1)S(1)}, bf16[1,64,3584]{2,1,0:T(8,128)(2,1)S(1)}, u32[]{:S(2)}, u32[]{:S(2)}) collective-permute-start(bf16[1,64,3584]{2,1,0:T(8,128)(2,1)S(1)} %fusion.29), channel_id=1, source_target_pairs={{0,16},{16,32},{32,48},{48,64},{64,80},{80,96},{96,112},{112,128},... | collective-permute-start | bytes 1376264 | tf_op jit(solution)/shard_map/ppermute | solution.py:16
  458.1 5.4 %collective-permute-done = bf16[1,64,3584]{2,1,0:T(8,128)(2,1)S(1)} collective-permute-done((bf16[1,64,3584]{2,1,0:T(8,128)(2,1)S(1)}, bf16[1,64,3584]{2,1,0:T(8,128)(2,1)S(1)}, u32[]{:S(2)}, u32[]{:S(2)}) %collective-permute-start) | collective-permute-done | bytes 458784 | tf_op jit(solution)/shard_map/ppermute | solution.py:16
  (106 shorter events, 29.6 us)
Async XLA Ops:
  0.6 126.8 %copy-start = (bf16[1,1,3584,256]{3,2,1,0:T(8,128)(2,1)S(1)}, bf16[1,1,3584,256]{3,2,1,0:T(8,128)(2,1)}, u32[]{:S(2)}) copy-start(bf16[1,1,3584,256]{3,2,1,0:T(8,128)(2,1)} %param.26) | copy-start | bytes 5505028
  3.5 6.5 %copy-start.15 = (bf16[1,64,2]{1,2,0:T(2,128)(2,1)S(1)}, bf16[1,64,2]{1,2,0:T(2,128)(2,1)}, u32[]{:S(2)}) copy-start(bf16[1,64,2]{1,2,0:T(2,128)(2,1)} %param.22) | copy-start | bytes 772
  3.6 6.5 %copy-start.12 = (s32[1,64,2]{1,2,0:T(2,128)S(1)}, s32[1,64,2]{1,2,0:T(2,128)}, u32[]{:S(2)}) copy-start(s32[1,64,2]{1,2,0:T(2,128)} %param.21) | copy-start | bytes 1540
  10.0 13.1 %copy-start.1 = (bf16[1,64,3584]{2,1,0:T(8,128)(2,1)S(1)}, bf16[1,64,3584]{2,1,0:T(8,128)(2,1)}, u32[]{:S(2)}) copy-start(bf16[1,64,3584]{2,1,0:T(8,128)(2,1)} %param.23) | copy-start | bytes 1376260
  12.3 19.2 %all-to-all-start.2 = ((bf16[16,1,32]{2,1,0:T(2,128)(2,1)}), bf16[16,1,32]{2,1,0:T(2,128)(2,1)S(1)}, u32[]{:S(2)}, u32[]{:S(2)}) async-start(bf16[16,1,32]{2,1,0:T(2,128)(2,1)} %copy.83), calls=%async_computation.2 | async-start | bytes 16384 | tf_op jit(solution)/shard_map/all_to_all | solution.py:112
  31.6 90.7 %all-to-all-start.3 = ((bf16[16,32,3584]{2,1,0:T(8,128)(2,1)}), bf16[16,32,3584]{2,1,0:T(8,128)(2,1)}, u32[]{:S(2)}, u32[]{:S(2)}) async-start(bf16[16,32,3584]{2,1,0:T(8,128)(2,1)} %broadcast_select_fusion), calls=%async_computation.3 | async-start | bytes 7340032 | tf_op jit(solution)/shard_map/all_to_all | solution.py:111
  122.2 3.9 copy-start.8
  122.2 3.9 copy-start.10
  122.2 3.9 copy-start.11
  130.5 9.1 %copy-start.13 = (s32[1,64,2]{1,2,0:T(2,128)S(1)}, s32[1,64,2]{1,2,0:T(2,128)}, u32[]{:S(2)}) copy-start(s32[1,64,2]{1,2,0:T(2,128)} %param.18) | copy-start | bytes 1540
  130.5 90.0 %all-to-all-start.4 = ((bf16[16,32,3584]{2,1,0:T(8,128)(2,1)}), bf16[16,32,3584]{2,1,0:T(8,128)(2,1)}, u32[]{:S(2)}, u32[]{:S(2)}) async-start(bf16[16,32,3584]{2,1,0:T(8,128)(2,1)} %bitcast.125), calls=%async_computation.4 | async-start | bytes 7340032 | tf_op jit(solution)/shard_map/all_to_all | solution.py:125
  140.2 6.5 %copy-start.14 = (bf16[1,3584]{1,0:T(2,128)(2,1)S(1)}, bf16[1,3584]{1,0:T(2,128)(2,1)}, u32[]{:S(2)}) copy-start(bf16[1,3584]{1,0:T(2,128)(2,1)} %param.24) | copy-start | bytes 21508
  140.2 6.6 %copy-start.4 = (bf16[1,64,3584]{2,1,0:T(8,128)(2,1)S(1)}, bf16[1,64,3584]{2,1,0:T(8,128)(2,1)}, u32[]{:S(2)}) copy-start(bf16[1,64,3584]{2,1,0:T(8,128)(2,1)} %param.17) | copy-start | bytes 1376260
  232.5 5.3 %copy-start.6 = (bf16[1,64,3584]{2,1,0:T(8,128)(2,1)S(1)}, bf16[1,64,3584]{2,1,0:T(8,128)(2,1)}, u32[]{:S(2)}) copy-start(bf16[1,64,3584]{2,1,0:T(8,128)(2,1)} %param.20) | copy-start | bytes 1376260
  236.9 0.9 copy-start.2
  244.8 93.3 %copy-start.9 = (bf16[1,1,3584,256]{3,2,1,0:T(8,128)(2,1)S(1)}, bf16[1,1,3584,256]{3,2,1,0:T(8,128)(2,1)}, u32[]{:S(2)}) copy-start(bf16[1,1,3584,256]{3,2,1,0:T(8,128)(2,1)} %param.25) | copy-start | bytes 5505028
  336.3 1.8 copy-start.7
  347.6 7.1 %copy-start.16 = (bf16[1,64,2]{1,2,0:T(2,128)(2,1)S(1)}, bf16[1,64,2]{1,2,0:T(2,128)(2,1)}, u32[]{:S(2)}) copy-start(bf16[1,64,2]{1,2,0:T(2,128)(2,1)} %param.19) | copy-start | bytes 772
  347.6 7.3 %copy-start.3 = (f32[64,3584]{1,0:T(8,128)S(1)}, f32[64,3584]{1,0:T(8,128)}, u32[]{:S(2)}) copy-start(f32[64,3584]{1,0:T(8,128)} %copy-done.2) | copy-start | bytes 2752516
  347.6 88.0 %all-to-all-start.1 = ((bf16[16,32,3584]{2,1,0:T(8,128)(2,1)}), bf16[16,32,3584]{2,1,0:T(8,128)(2,1)}, u32[]{:S(2)}, u32[]{:S(2)}) async-start(bf16[16,32,3584]{2,1,0:T(8,128)(2,1)} %bitcast.126), calls=%async_computation.1 | async-start | bytes 7340032 | tf_op jit(solution)/shard_map/all_to_all | solution.py:103
  356.9 101.1 %collective-permute-start.1 = (bf16[1,64,3584]{2,1,0:T(8,128)(2,1)}, bf16[1,64,3584]{2,1,0:T(8,128)(2,1)S(1)}, u32[]{:S(2)}, u32[]{:S(2)}) collective-permute-start(bf16[1,64,3584]{2,1,0:T(8,128)(2,1)} %fusion.37), channel_id=1, source_target_pairs={{16,0},{32,16},{48,32},{64,48},{80,64},{96,80},{112,96},{128,112},... | collective-permute-start | bytes 1376264 | tf_op jit(solution)/shard_map/ppermute | solution.py:16
  447.6 4.8 %copy-start.5 = (bf16[1,64,3584]{2,1,0:T(8,128)(2,1)S(1)}, bf16[1,64,3584]{2,1,0:T(8,128)(2,1)}, u32[]{:S(2)}) copy-start(bf16[1,64,3584]{2,1,0:T(8,128)(2,1)} %param.17) | copy-start | bytes 1376260
  452.5 11.0 %collective-permute-start = (bf16[1,64,3584]{2,1,0:T(8,128)(2,1)S(1)}, bf16[1,64,3584]{2,1,0:T(8,128)(2,1)S(1)}, u32[]{:S(2)}, u32[]{:S(2)}) collective-permute-start(bf16[1,64,3584]{2,1,0:T(8,128)(2,1)S(1)} %fusion.29), channel_id=1, source_target_pairs={{0,16},{16,32},{32,48},{48,64},{64,80},{80,96},{96,112},{112,128},... | collective-permute-start | bytes 1376264 | tf_op jit(solution)/shard_map/ppermute | solution.py:16
where the time goes:
time: 471 us; the launch traced here: 465 us
  waiting for transfers between devices  233 us (49%)
  blocking collectives  91.5 us (19%)
  local copies, waits for them, and re-layouts  45.7 us (10%)
  starting transfers between devices  45.2 us (10%)
  other arithmetic  30.5 us (6%)
  matrix products  17.7 us (4%)
    all_to_all x1, blocking collectives, body(): lax.all_to_all(outgoing_fwd, 'expert', split_axis=0, concat_axis=0, tiled...  91.5 us
    all_to_all x1, waiting for transfers between devices, body(): lax.all_to_all(outgoing_cot, 'expert', split_axis=0, concat_axis=0, tiled...  81.5 us
    all_to_all x1, waiting for transfers between devices, body(): lax.all_to_all(partial_value.reshape(arrived.shape[0], arrived.shape[1],...  74.2 us
    all_to_all x1, waiting for transfers between devices, body(): lax.all_to_all(partial_value.reshape(cot_arrived.shape[0], cot_arrived.sh...  72.3 us
    gather x4, local copies, waits for them, and re-layouts, combine_rows(): return jnp.take(flat_rows, expert_ids * CAP + slot_of, axis=0)  15.9 us
    scatter x2, local copies, waits for them, and re-layouts, route_tables(): jnp.zeros((EXPERTS, CAP), jnp.int32).at[expert_ids, slot_of].set(positions)  12.8 us
    all_to_all x1, starting transfers between devices, body(): lax.all_to_all(weight_out, 'expert', split_axis=0, concat_axis=0, tiled=T...  10.7 us
    ppermute x2, starting transfers between devices, from_behind(): lax.ppermute(value, axis, [(source, source + steps) for source in range(l...  9.98 us
  transfers between devices with their start and end apart: 6, of which 4 were waited for; matrix products, arithmetic and copies ran while one was open for 8% of the time, Pallas kernels for 0%

commit v1 on v0

v1 whole, which is shorter than its diff:
```python
import jax
import jax.numpy as jnp
from jax import lax
from jax.experimental import pallas as pl
from jax.experimental.pallas import tpu as pltpu
from jax.sharding import PartitionSpec as P

MESH = pl.DeviceIdType.MESH
D = 3584
FF = 256
TOK = 64
CAP = 32
HALF = 128
FULL = 256
COLS = 512
CHUNKS = D // COLS
EPS = 1e-06
F32 = jnp.float32
BF16 = jnp.bfloat16


def dot(left, right):
    return lax.dot_general(left, right, (((1,), (0,)), ((), ())), preferred_element_type=F32)


def dot_nt(left, right):
    return lax.dot_general(left, right, (((1,), (1,)), ((), ())), preferred_element_type=F32)


def rows(ref, slot, count=1):
    return ref.at[pl.ds(slot * CAP, count * CAP), :]


def selection(ids, slot_experts):
    lane = lax.broadcasted_iota(jnp.int32, (TOK, HALF), 1)
    slot = lax.shift_right_logical(lane, 5)
    rank_of = (lane & (CAP - 1)).astype(F32)
    expert = jnp.zeros((TOK, HALF), jnp.int32)
    for s, e in enumerate(slot_experts):
        expert = jnp.where(slot == s, e, expert)
    first = ids[:, 0:1] == expert
    second = ids[:, 1:2] == expert
    named = jnp.where(first | second, 1.0, 0.0)
    below = lax.broadcasted_iota(jnp.int32, (TOK, TOK), 1) < lax.broadcasted_iota(
        jnp.int32, (TOK, TOK), 0
    )
    ranks = dot(jnp.where(below, 1.0, 0.0).astype(BF16), named.astype(BF16))
    hit = ranks == rank_of
    return first & hit, second & hit


def weigh(masks, weights):
    first, second = masks
    return jnp.where(first, weights[:, 0:1], 0.0) + jnp.where(second, weights[:, 1:2], 0.0)


def kernel(
    fids, fw, bids, bw, gain, xf_h, xb_h, ct_h, wg_h, wu_h, wd_h, sg_h, su_h,
    nxt, prv,
    xf, xb, ct, wg, wu, wd, wdo, sg, su,
    csend, fsend, crow, frow,
    dho, dsend, drecv, dg, du,
    bsend, brecv, bown, zsb, zrb, zdb, retb,
    hown, hsend, hrecv, zsf, zrf, zdf, retf,
    fout, gout, dn,
    ld, s_wd, r_wd, s_c, r_c, s_f, r_f, s_fy, r_fy, s_d, r_d, s_by, r_by,
    s_bp, r_bp, s_bd, r_bd, s_h, r_h, s_fp, r_fp, s_fd, r_fd, s_out, r_out,
):
    p = lax.axis_index("pipe")
    me = lax.axis_index("expert")
    z = lax.div(me, 2)
    y = lax.rem(me, 2)
    dz = 2 * lax.rem(z, 2) - 1

    def at_z(zz):
        return lax.rem(zz + 8, 8)

    def dev(zz):
        return (p, at_z(zz) * 2 + y)

    targets = [z, z + dz, z - 2 * dz, z + 3 * dz]
    sources = [z, z + dz, z + 2 * dz, z + 3 * dz]
    pz = z - dz
    partner = dev(pz)
    y_partner = (p, z * 2 + 1 - y)
    slot_experts = [lax.div(at_z(t), 2) for t in targets]
    block_z = [at_z(s) for s in sources] + [at_z(pz - k * dz) for k in range(4)]

    barrier = pltpu.get_barrier_semaphore()
    friends = [
        partner,
        dev(z + dz),
        dev(z + 2 * dz),
        dev(z - 2 * dz),
        dev(z + 3 * dz),
        y_partner,
        (lax.rem(p + 1, 16), me),
        (lax.rem(p + 15, 16), me),
    ]
    for friend in friends:
        pl.semaphore_signal(barrier, inc=1, device_id=friend, device_id_type=MESH)

    loads = {}
    for i, (name, src, dst) in enumerate(
        [
            ("ct", ct_h, ct),
            ("xf", xf_h, xf),
            ("wd", wd_h, wd),
            ("wg", wg_h, wg),
            ("wu", wu_h, wu),
            ("sg", sg_h, sg),
            ("su", su_h, su),
            ("xb", xb_h, xb),
        ]
    ):
        loads[name] = pltpu.make_async_copy(src, dst, ld.at[i])
        loads[name].start()

    sent = []

    def remote(src, dst, s_sem, r_sem, target):
        return pltpu.make_async_remote_copy(
            src_ref=src, dst_ref=dst, send_sem=s_sem, recv_sem=r_sem,
            device_id=target, device_id_type=MESH,
        )

    def send(cp):
        cp.start()
        sent.append(cp)

    bmask = selection(bids[...], slot_experts)
    b_hot = weigh(bmask, jnp.ones((TOK, 2), F32)).astype(BF16)
    b_gather = weigh(bmask, bw[...].astype(F32)).T.astype(BF16)
    loads["ct"].wait()
    for c in range(CHUNKS):
        cs = slice(c * COLS, (c + 1) * COLS)
        csend[:, cs] = dot(b_gather, ct[:, cs]).astype(BF16)
    crow[0:CAP, :] = csend[0:CAP, :]

    pl.semaphore_wait(barrier, len(friends))

    wd_copies = [
        remote(wd_h.at[pl.ds(i * 64, 64), :], wdo.at[pl.ds(i * 64, 64), :], s_wd.at[i], r_wd.at[i], y_partner)
        for i in range(4)
    ]
    for cp in wd_copies:
        send(cp)

    def z_copies(block, out, s_sem, r_sem):
        cps = [None]
        for k in (1, 2, 3):
            cps.append(remote(rows(block, k), rows(out, k), s_sem.at[k], r_sem.at[k], dev(targets[k])))
        for k in range(4):
            cps.append(remote(rows(out, k), rows(out, 4 + k), s_sem.at[4 + k], r_sem.at[4 + k], partner))
        return cps

    c_cp = z_copies(csend, crow, s_c, r_c)
    for k in (3, 2, 1, 4):
        send(c_cp[k])

    fmask = selection(fids[...], slot_experts)
    f_hot = weigh(fmask, jnp.ones((TOK, 2), F32)).T.astype(BF16)
    f_weights = weigh(fmask, fw[...].astype(F32)).astype(BF16)
    gain_wide = gain[...].astype(F32)
    loads["xf"].wait()
    wide = xf[...].astype(F32)
    scale = lax.rsqrt(jnp.mean(wide * wide, axis=-1, keepdims=True) + EPS)
    fout[...] = (wide * scale * gain_wide).astype(BF16)
    for c in range(CHUNKS):
        cs = slice(c * COLS, (c + 1) * COLS)
        fsend[:, cs] = dot(f_hot, fout[:, cs]).astype(BF16)
    frow[0:CAP, :] = fsend[0:CAP, :]

    f_cp = z_copies(fsend, frow, s_f, r_f)
    fy_cp = [
        remote(rows(frow, j), rows(frow, 8 + j), s_fy.at[j], r_fy.at[j], y_partner) for j in range(8)
    ]

    for k in (1, 2, 3):
        c_cp[k].wait_recv()
        send(c_cp[4 + k])
    for k in (3, 2, 1, 4):
        send(f_cp[k])

    loads["wd"].wait()
    dho[0:HALF, :] = dot_nt(crow[0:HALF, :], wd[...])
    for k in range(4):
        c_cp[4 + k].wait_recv()
    dho[HALF:FULL, :] = dot_nt(crow[HALF:FULL, :], wd[...])

    send(fy_cp[0])
    f_cp[1].wait_recv()
    send(f_cp[5])
    send(fy_cp[1])

    for cp in wd_copies:
        cp.wait_recv()
    dsend[...] = dot_nt(crow[...], wdo[...]).astype(BF16)
    d_cp = remote(dsend, drecv, s_d.at[0], r_d.at[0], y_partner)
    send(d_cp)

    for k in (2, 3):
        f_cp[k].wait_recv()
        send(f_cp[4 + k])
        send(fy_cp[k])

    loads["sg"].wait()
    loads["su"].wait()

    def activation_grad(j, column, d_hidden):
        start = pl.multiple_of((block_z[j] * 2 + column) * CAP, CAP)
        gate_b = sg[pl.ds(start, CAP), :].astype(F32)
        up_b = su[pl.ds(start, CAP), :].astype(F32)
        sigmoid = jax.nn.sigmoid(gate_b)
        d_gate = d_hidden * up_b * sigmoid * (1.0 + gate_b * (1.0 - sigmoid))
        d_up = d_hidden * gate_b * sigmoid
        return d_gate.astype(BF16), d_up.astype(BF16)

    for j in range(8):
        js = slice(j * CAP, (j + 1) * CAP)
        d_gate, d_up = activation_grad(j, y, dho[js, :])
        dg[js, :] = d_gate
        du[js, :] = d_up
    d_cp.wait_recv()
    for j in range(8):
        js = slice(j * CAP, (j + 1) * CAP)
        ks = slice(FULL + j * CAP, FULL + (j + 1) * CAP)
        d_gate, d_up = activation_grad(j, 1 - y, drecv[js, :].astype(F32))
        dg[ks, :] = d_gate
        du[ks, :] = d_up

    loads["wg"].wait()
    loads["wu"].wait()
    by_cp = [remote(rows(bsend, j), rows(brecv, j), s_by.at[j], r_by.at[j], y_partner) for j in range(8)]
    for c in range(CHUNKS):
        cs = slice(c * COLS, (c + 1) * COLS)
        bsend[:, cs] = (
            dot_nt(dg[FULL : 2 * FULL, :], wg[cs, :]) + dot_nt(du[FULL : 2 * FULL, :], wu[cs, :])
        ).astype(BF16)
    for k in range(4):
        send(by_cp[4 + k])
        send(by_cp[k])
    for c in range(CHUNKS):
        cs = slice(c * COLS, (c + 1) * COLS)
        bown[:, cs] = dot_nt(dg[0:FULL, :], wg[cs, :]) + dot_nt(du[0:FULL, :], wu[cs, :])

    def hidden(block):
        gate = dot(block, wg[...])
        up = dot(block, wu[...])
        return (gate * jax.nn.sigmoid(gate) * up).astype(BF16)

    for k in range(4):
        f_cp[4 + k].wait_recv()
    hown[...] = hidden(frow[0:FULL, :])

    h_cp = [
        remote(rows(hsend, 4 * g, 4), rows(hrecv, 4 * g, 4), s_h.at[g], r_h.at[g], y_partner) for g in range(2)
    ]

    def partner_hidden(g):
        for j in range(4 * g, 4 * g + 4):
            fy_cp[j].wait_recv()
        hsend[g * HALF : (g + 1) * HALF, :] = hidden(frow[FULL + g * HALF : FULL + (g + 1) * HALF, :])
        send(h_cp[g])

    partner_hidden(0)

    bp_cp = [remote(rows(zsb, k), rows(zrb, k), s_bp.at[k], r_bp.at[k], partner) for k in range(4)]
    bd_cp = [None] + [
        remote(rows(zdb, k), rows(retb, k), s_bd.at[k], r_bd.at[k], dev(sources[k])) for k in (1, 2, 3)
    ]
    for k in range(4):
        ks = slice(k * CAP, (k + 1) * CAP)
        js = slice(HALF + k * CAP, HALF + (k + 1) * CAP)
        by_cp[4 + k].wait_recv()
        zsb[ks, :] = (bown[js, :] + brecv[js, :].astype(F32)).astype(BF16)
        send(bp_cp[k])
        if k == 1:
            for m in range(4):
                send(fy_cp[4 + m])
    for k in (3, 2, 1, 0):
        ks = slice(k * CAP, (k + 1) * CAP)
        by_cp[k].wait_recv()
        bp_cp[k].wait_recv()
        total = (bown[ks, :] + brecv[ks, :].astype(F32) + zrb[ks, :].astype(F32)).astype(BF16)
        if k == 0:
            retb[ks, :] = total
        else:
            zdb[ks, :] = total
            send(bd_cp[k])

    fp_cp = [remote(rows(zsf, k), rows(zrf, k), s_fp.at[k], r_fp.at[k], partner) for k in range(4)]
    fd_cp = [None] + [
        remote(rows(zdf, k), rows(retf, k), s_fd.at[k], r_fd.at[k], dev(sources[k])) for k in (1, 2, 3)
    ]
    partner_hidden(1)
    h_cp[1].wait_recv()
    for c in range(CHUNKS):
        cs = slice(c * COLS, (c + 1) * COLS)
        zsf[:, cs] = (
            dot(hown[HALF:FULL, :], wd[:, cs]) + dot(hrecv[HALF:FULL, :], wdo[:, cs])
        ).astype(BF16)
    for k in (3, 2, 1, 0):
        send(fp_cp[k])

    for k in (1, 2, 3):
        bd_cp[k].wait_recv()
    loads["xb"].wait()
    wide_b = xb[...].astype(F32)
    scale_b = lax.rsqrt(jnp.mean(wide_b * wide_b, axis=-1, keepdims=True) + EPS)
    inner = jnp.zeros((TOK, 1), F32)
    for c in range(CHUNKS):
        cs = slice(c * COLS, (c + 1) * COLS)
        part = dot(b_hot, retb[:, cs]) * gain_wide[:, cs]
        dn[:, cs] = part
        inner = inner + jnp.sum(part * (xb[:, cs].astype(F32) * scale_b), axis=-1, keepdims=True)
    inner = inner * (1.0 / D)
    for c in range(CHUNKS):
        cs = slice(c * COLS, (c + 1) * COLS)
        unit = xb[:, cs].astype(F32) * scale_b
        gout[:, cs] = (ct[:, cs].astype(F32) + scale_b * (dn[:, cs] - unit * inner)).astype(BF16)
    b_out = remote(gout, prv, s_out.at[1], r_out.at[1], (lax.rem(p + 15, 16), me))

    @pl.when(p > 0)
    def _():
        b_out.start()

    h_cp[0].wait_recv()
    for c in range(CHUNKS):
        cs = slice(c * COLS, (c + 1) * COLS)
        bown[0:HALF, cs] = dot(hown[0:HALF, :], wd[:, cs]) + dot(hrecv[0:HALF, :], wdo[:, cs])
    for k in (3, 2, 1, 0):
        ks = slice(k * CAP, (k + 1) * CAP)
        fp_cp[k].wait_recv()
        total = (bown[ks, :] + zrf[ks, :].astype(F32)).astype(BF16)
        if k == 0:
            retf[ks, :] = total
        else:
            zdf[ks, :] = total
            send(fd_cp[k])
    for k in (1, 2, 3):
        fd_cp[k].wait_recv()
    for c in range(CHUNKS):
        cs = slice(c * COLS, (c + 1) * COLS)
        fout[:, cs] = (xf[:, cs].astype(F32) + dot(f_weights, retf[:, cs])).astype(BF16)
    f_out = remote(fout, nxt, s_out.at[0], r_out.at[0], (lax.rem(p + 1, 16), me))

    @pl.when(p < 15)
    def _():
        f_out.start()

    @pl.when(p == 0)
    def _():
        gout[...] = jnp.zeros_like(gout)
        zero = pltpu.make_async_copy(gout, nxt, ld.at[8])
        zero.start()
        zero.wait()

    @pl.when(p == 15)
    def _():
        fout[...] = jnp.zeros_like(fout)
        zero = pltpu.make_async_copy(fout, prv, ld.at[9])
        zero.start()
        zero.wait()

    for cp in sent:
        cp.wait_send()

    @pl.when(p > 0)
    def _():
        f_out.wait_recv()
        b_out.wait_send()

    @pl.when(p < 15)
    def _():
        b_out.wait_recv()
        f_out.wait_send()


def body(
    fwd_rows,
    fwd_experts,
    fwd_weight,
    back_rows,
    back_experts,
    back_weight,
    back_cotangent,
    norm_gain,
    w_gate,
    w_up,
    w_down,
    saved_gate,
    saved_up,
):
    vmem = pl.BlockSpec(memory_space=pltpu.VMEM)
    hbm = pl.BlockSpec(memory_space=pl.ANY)
    dma = pltpu.SemaphoreType.DMA

    def wide(count, kind=BF16):
        return pltpu.VMEM((count, D), kind)

    def narrow(count, kind=BF16):
        return pltpu.VMEM((count, FF), kind)

    outs = pl.pallas_call(
        kernel,
        out_shape=(jax.ShapeDtypeStruct((TOK, D), BF16), jax.ShapeDtypeStruct((TOK, D), BF16)),
        in_specs=[vmem] * 5 + [hbm] * 8,
        out_specs=(hbm, hbm),
        scratch_shapes=[
            wide(TOK), wide(TOK), wide(TOK),
            narrow(D), narrow(D), wide(FF), wide(FF), narrow(512), narrow(512),
            wide(HALF), wide(HALF), wide(FULL), wide(2 * FULL),
            narrow(FULL, F32), narrow(FULL), narrow(FULL), narrow(512), narrow(512),
            wide(FULL), wide(FULL), wide(FULL, F32), wide(HALF), wide(HALF), wide(HALF), wide(HALF),
            narrow(FULL), narrow(FULL), narrow(FULL), wide(HALF), wide(HALF), wide(HALF), wide(HALF),
            wide(TOK), wide(TOK), wide(TOK, F32),
            dma((10,)), dma((4,)), dma((4,)), dma((8,)), dma((8,)), dma((8,)), dma((8,)),
            dma((8,)), dma((8,)), dma((1,)), dma((1,)), dma((8,)), dma((8,)),
            dma((4,)), dma((4,)), dma((4,)), dma((4,)), dma((2,)), dma((2,)),
            dma((4,)), dma((4,)), dma((4,)), dma((4,)), dma((2,)), dma((2,)),
        ],
        compiler_params=pltpu.CompilerParams(
            collective_id=0, has_side_effects=True, vmem_limit_bytes=56 * 2**20
        ),
        cost_estimate=pl.CostEstimate(flops=5_700_000_000, bytes_accessed=10_000_000, transcendentals=400_000),
    )(
        fwd_experts[0],
        fwd_weight[0],
        back_experts[0],
        back_weight[0],
        norm_gain,
        fwd_rows[0],
        back_rows[0],
        back_cotangent[0],
        w_gate[0, 0],
        w_up[0, 0],
        w_down[0, 0],
        saved_gate[0, 0],
        saved_up[0, 0],
    )
    return outs[0][None], outs[1][None]


def solution(mesh):
    rows3 = P("pipe", "expert", None)
    rows4 = P("pipe", "expert", None, None)
    placed = (rows3,) * 7 + (P("pipe", None),) + (rows4,) * 5
    return jax.shard_map(
        body,
        mesh=mesh,
        in_specs=placed,
        out_specs=(rows3, rows3),
        check_vma=False,
    )
```

time: 471 us -> 188 us (0.40)
  waiting for transfers between devices: 233 us -> 0 us
  Pallas kernels: 0 us -> 175 us
  blocking collectives: 91.5 us -> 0 us
  starting transfers between devices: 45.2 us -> 0 us
  local copies, waits for them, and re-layouts: 45.7 us -> 9.09 us
  other arithmetic: 30.5 us -> 0 us
  matrix products: 17.7 us -> 0 us
    all_to_all x4 -> x0, waiting for transfers between devices: 228 us -> none  [the longest x1 81.5 us: body(): lax.all_to_all(outgoing_cot, 'expert', split_axis=0, concat_axis=0, tiled...]
    pallas_call x0 -> x1, Pallas kernels: none -> 175 us  [body(): pl.pallas_call(kernel, out_shape=(jax.ShapeDtypeStruct((TOK, D), BF16), j...]
    all_to_all x1 -> x0, blocking collectives: 91.5 us -> none  [body(): lax.all_to_all(outgoing_fwd, 'expert', split_axis=0, concat_axis=0, tiled...]
    all_to_all x4 -> x0, starting transfers between devices: 35.2 us -> none  [the longest x1 10.7 us: body(): lax.all_to_all(weight_out, 'expert', split_axis=0, concat_axis=0, tiled=T...]
    gather x7 -> x0, local copies, waits for them, and re-layouts: 25.8 us -> none  [the longest x4 15.9 us: combine_rows(): return jnp.take(flat_rows, expert_ids * CAP + slot_of, axis=0)]
    reduce_sum x12 -> x0, other arithmetic: 20.6 us -> none  [the longest x2 8.13 us: combine_rows(): jnp.sum(returned.reshape(EXPERTS, split_count, CAP, width), axis=1, dtype...]
    dot_general x5 -> x0, matrix products: 17.7 us -> none  [the longest x1 8.38 us: body(): jnp.dot(hidden_f, down_mat, preferred_element_type=jnp.float32)]
    scatter x2 -> x0, local copies, waits for them, and re-layouts: 12.8 us -> none  [route_tables(): jnp.zeros((EXPERTS, CAP), jnp.int32).at[expert_ids, slot_of].set(positions)]
  transfers between devices with their start and end apart: 6 -> 0, of which waited for: 4 -> 0; matrix products, arithmetic and copies ran while one was open for 8% -> 0% of each run, Pallas kernels for 0% -> 0%
where the time goes in v1:
time: 188 us; the launch traced here: 185 us
  Pallas kernels  175 us (93%)
  local copies, waits for them, and re-layouts  9.09 us (5%)
    pallas_call x1, Pallas kernels, body(): pl.pallas_call(kernel, out_shape=(jax.ShapeDtypeStruct((TOK, D), BF16), j...  175 us

profile of v1, /device:TPU:37, one launch (start us, length us, event | category | flops | bytes accessed | tf_op | source)
XLA Modules:
  0.0 184.7 jit_solution(16596269512363837011)
XLA Ops:
  0.6 1.4 copy.16.fw
  2.0 1.3 copy.18.bw
  3.3 1.4 copy.15.fids
  4.7 1.4 copy.17.bids
  6.1 175.0 %shard_map.140 = (bf16[64,3584]{1,0:T(8,128)(2,1)}, bf16[64,3584]{1,0:T(8,128)(2,1)}) custom-call(s32[64,2]{1,0:T(8,128)} %copy.15.fids, bf16[64,2]{1,0:T(8,128)(2,1)} %copy.16.fw, s32[64,2]{1,0:T(8,128)} %copy.17.bids, bf16[64,2]{1,0:T(8,128)(2,1)} %copy.18.bw, bf16[1,3584]{1,0:T(2,128)(2,1)} %gain.1, bf16[64,3584]{1,0:T(8,128)(2,1)} %bitcast.23, ...), custom_call_target="tpu_custom_call" | custom-call | flops 5699999744 | bytes 10000000 | tf_op jit(solution)/shard_map/pallas_call | solution.py:405
  181.1 1.8 copy.21
  182.9 1.8 copy.22

commit v2 on v1

v2 whole, which is shorter than its diff:
```python
import jax
import jax.numpy as jnp
from jax import lax
from jax.experimental import pallas as pl
from jax.experimental.pallas import tpu as pltpu
from jax.sharding import PartitionSpec as P

MESH = pl.DeviceIdType.MESH
D = 3584
FF = 256
TOK = 64
CAP = 32
HALF = 128
FULL = 256
COLS = 512
CHUNKS = [slice(c, c + COLS) for c in range(0, D, COLS)]
W_PARTS = 8
EPS = 1e-06
F32 = jnp.float32
BF16 = jnp.bfloat16

ORDER = [
    "~prepC", "+C4", "+C1", "+W0", "+W1", "+W2", "+W3", "~prepF", "+F2", "+F3", "+W4", "+W5", "?C1",
    "+W6", "+F4", "+W7", "?F3", "+Y3", "?F2", "+F6", "+F7", "+C2", "+F1", "?W0", "?F1", "+F5",
    "?F6", "+Y6", "+C3", "?W1", "?W2", "?F7", "?W3", "?C2", "+Y2", "+C6", "?W4", "?F4", "+Y7",
    "+C5", "?W5", "?W6", "?Y6", "?C3", "+C7", "?F5", "?Y3", "?Y2", "~h2", "+H2", "+Y1", "?C5",
    "?Y7", "~h3", "+H3", "~hown", "?W7", "+Y5", "?H2", "~fo2", "+FP2", "?C6", "?H3", "~fo3", "+FP3",
    "+Y0", "?FP2", "~fa2", "+FD2", "?C7", "?C4", "?Y1", "?Y5", "~h1", "+H1", "~dhoth", "+D", "?FP3",
    "~fa3", "+FD3", "+Y4", "?H1", "~fo1", "?Y0", "+FP1", "?D", "~bs", "+G7", "~dhown", "~actown",
    "?Y4", "~h0", "+H0", "+G5", "+G3", "~bown", "+G6", "?G7", "~ba3", "+G4", "+BP3", "?FD2", "?H0",
    "~fo0", "+FP0", "?G5", "~ba1", "?FP1", "?BP3", "+BP1", "~fa1", "?G3", "+FD1", "?FP0", "+G1",
    "~bb3", "+BD3", "?G6", "?FD3", "~ba2", "+G2", "+BP2", "?G4", "?BP1", "~ba0", "+BP0", "?G1",
    "~bb1", "+G0", "+BD1", "?G2", "?BP2", "~bb2", "+BD2", "?BD3", "?FD1", "?BP0", "~fa0", "~cf",
    "+RF", "?G0", "~bb0", "?BD1", "?BD2", "~cb", "+RB", "?RF", "?RB"
]


def dot(left, right):
    return lax.dot_general(left, right, (((1,), (0,)), ((), ())), preferred_element_type=F32)


def dot_nt(left, right):
    return lax.dot_general(left, right, (((1,), (1,)), ((), ())), preferred_element_type=F32)


def place(slot):
    return 2 * (slot % 4) + slot // 4


def span(position, count=1, base=0):
    return slice(base + position * CAP, base + (position + count) * CAP)


def rows(ref, position, count=1):
    return ref.at[pl.ds(position * CAP, count * CAP), :]


def selection(ids, slot_experts):
    line = lax.broadcasted_iota(jnp.int32, (HALF, TOK), 0)
    slot = lax.shift_right_logical(line, 5)
    rank_of = (line & (CAP - 1)).astype(F32)
    expert = jnp.zeros((HALF, TOK), jnp.int32)
    for s, e in enumerate(slot_experts):
        expert = jnp.where(slot == s, e, expert)
    first = ids[0:1, :] == expert
    second = ids[1:2, :] == expert
    named = jnp.where(first | second, 1.0, 0.0)
    before = lax.broadcasted_iota(jnp.int32, (TOK, TOK), 0) < lax.broadcasted_iota(
        jnp.int32, (TOK, TOK), 1
    )
    ranks = dot(named.astype(BF16), jnp.where(before, 1.0, 0.0).astype(BF16))
    hit = ranks == rank_of
    return first & hit, second & hit


def weigh(masks, weights):
    first, second = masks
    return jnp.where(first, weights[0:1, :], 0.0) + jnp.where(second, weights[1:2, :], 0.0)


def kernel(
    fids, fw, bids, bw, gain, xf_h, xb_h, ct_h, wg_h, wu_h, wd_h, sg_h, su_h,
    nxt, prv,
    xf, xb, ct, wg, wu, wd, wdo, sg, su,
    csend, fsend, crow, frow,
    dho, dsend, drecv, dg, du,
    bsend, brecv, bown, zsb, zrb, zdb, retb,
    hown, hsend, hrecv, fown, zsf, zrf, zdf, retf,
    fout, gout, dn, b_hot, f_hot,
    ld, s_w, r_w, s_c, r_c, s_f, r_f, s_y, r_y, s_d, r_d, s_g, r_g,
    s_bp, r_bp, s_bd, r_bd, s_h, r_h, s_fp, r_fp, s_fd, r_fd, s_out, r_out,
):
    p = lax.axis_index("pipe")
    me = lax.axis_index("expert")
    z = lax.div(me, 2)
    y = lax.rem(me, 2)
    dz = 2 * lax.rem(z, 2) - 1

    def at_z(zz):
        return lax.rem(zz + 8, 8)

    def dev(zz):
        return (p, at_z(zz) * 2 + y)

    targets = [z, z + dz, z - 2 * dz, z + 3 * dz]
    sources = [z, z + dz, z + 2 * dz, z + 3 * dz]
    pz = z - dz
    z_partner = dev(pz)
    y_partner = (p, z * 2 + 1 - y)
    later = (lax.rem(p + 1, 16), me)
    earlier = (lax.rem(p + 15, 16), me)
    slot_experts = [lax.div(at_z(t), 2) for t in targets]
    block_z = [at_z(s) for s in sources] + [at_z(pz - k * dz) for k in range(4)]

    barrier = pltpu.get_barrier_semaphore()
    friends = [
        z_partner,
        dev(z + dz),
        dev(z + 2 * dz),
        dev(z - 2 * dz),
        dev(z + 3 * dz),
        y_partner,
        later,
        earlier,
    ]
    for friend in friends:
        pl.semaphore_signal(barrier, inc=1, device_id=friend, device_id_type=MESH)

    loads = {}
    for i, (name, src, dst) in enumerate(
        [
            ("ct", ct_h, ct),
            ("xf", xf_h, xf),
            ("wd", wd_h, wd),
            ("wg", wg_h, wg),
            ("wu", wu_h, wu),
            ("sg", sg_h, sg),
            ("su", su_h, su),
            ("xb", xb_h, xb),
        ]
    ):
        loads[name] = pltpu.make_async_copy(src, dst, ld.at[i])
        loads[name].start()

    def need(*names):
        for name in names:
            if name in loads:
                loads.pop(name).wait()

    copies = {}

    def remote(name, src, dst, s_sem, r_sem, target):
        copies[name] = pltpu.make_async_remote_copy(
            src_ref=src, dst_ref=dst, send_sem=s_sem, recv_sem=r_sem,
            device_id=target, device_id_type=MESH,
        )

    part = FF // W_PARTS
    for i in range(W_PARTS):
        cut = pl.ds(i * part, part)
        remote(f"W{i}", wd_h.at[cut, :], wdo.at[cut, :], s_w.at[i], r_w.at[i], y_partner)
    for name, block, out, s_sem, r_sem in (("C", csend, crow, s_c, r_c), ("F", fsend, frow, s_f, r_f)):
        for k in (1, 2, 3):
            remote(
                f"{name}{k}", rows(block, k), rows(out, place(k)), s_sem.at[k], r_sem.at[k], dev(targets[k])
            )
        for k in range(4):
            remote(
                f"{name}{4 + k}", rows(out, place(k)), rows(out, place(4 + k)),
                s_sem.at[4 + k], r_sem.at[4 + k], z_partner,
            )
    for j in range(8):
        remote(f"Y{j}", rows(frow, place(j)), rows(frow, 8 + place(j)), s_y.at[j], r_y.at[j], y_partner)
        remote(f"G{j}", rows(bsend, place(j)), rows(brecv, place(j)), s_g.at[j], r_g.at[j], y_partner)
    remote("D", dsend, drecv, s_d.at[0], r_d.at[0], y_partner)
    for k in range(4):
        remote(f"H{k}", rows(hsend, 2 * k, 2), rows(hrecv, 2 * k, 2), s_h.at[k], r_h.at[k], y_partner)
        remote(f"BP{k}", rows(zsb, k), rows(zrb, k), s_bp.at[k], r_bp.at[k], z_partner)
        remote(f"FP{k}", rows(zsf, k), rows(zrf, k), s_fp.at[k], r_fp.at[k], z_partner)
    for k in (1, 2, 3):
        remote(f"BD{k}", rows(zdb, k), rows(retb, k), s_bd.at[k], r_bd.at[k], dev(sources[k]))
        remote(f"FD{k}", rows(zdf, k), rows(retf, k), s_fd.at[k], r_fd.at[k], dev(sources[k]))
    remote("RF", fout, nxt, s_out.at[0], r_out.at[0], later)
    remote("RB", gout, prv, s_out.at[1], r_out.at[1], earlier)

    computed = {}

    def compute(name, function, *given):
        computed[name] = (function, given)

    def cotangent_blocks():
        masks = selection(bids[...], slot_experts)
        b_hot[...] = weigh(masks, jnp.ones((2, TOK), F32)).T.astype(BF16)
        gather = weigh(masks, bw[...].astype(F32)).astype(BF16)
        need("ct")
        for cs in CHUNKS:
            csend[:, cs] = dot(gather, ct[:, cs]).astype(BF16)
        crow[span(0), :] = csend[span(0), :]
        pl.semaphore_wait(barrier, len(friends))

    def forward_blocks():
        masks = selection(fids[...], slot_experts)
        gather = weigh(masks, jnp.ones((2, TOK), F32)).astype(BF16)
        f_hot[...] = weigh(masks, fw[...].astype(F32)).T.astype(BF16)
        need("xf")
        wide = xf[...].astype(F32)
        scale = lax.rsqrt(jnp.mean(wide * wide, axis=-1, keepdims=True) + EPS)
        fout[...] = (wide * scale * gain[...].astype(F32)).astype(BF16)
        for cs in CHUNKS:
            fsend[:, cs] = dot(gather, fout[:, cs]).astype(BF16)
        frow[span(0), :] = fsend[span(0), :]

    def own_d_hidden():
        need("wd")
        dho[...] = dot_nt(crow[...], wd[...])

    def other_d_hidden():
        dsend[...] = dot_nt(crow[...], wdo[...]).astype(BF16)

    def activation_grad(j, column, d_hidden):
        need("sg", "su")
        start = pl.multiple_of((block_z[j] * 2 + column) * CAP, CAP)
        gate_b = sg[pl.ds(start, CAP), :].astype(F32)
        up_b = su[pl.ds(start, CAP), :].astype(F32)
        sigmoid = jax.nn.sigmoid(gate_b)
        d_gate = d_hidden * up_b * sigmoid * (1.0 + gate_b * (1.0 - sigmoid))
        d_up = d_hidden * gate_b * sigmoid
        return d_gate.astype(BF16), d_up.astype(BF16)

    def own_activation():
        for j in range(8):
            js = span(place(j))
            dg[js, :], du[js, :] = activation_grad(j, y, dho[js, :])

    def other_gradient():
        need("wg", "wu")
        for j in range(8):
            js = span(place(j))
            ks = span(place(j), 1, FULL)
            dg[ks, :], du[ks, :] = activation_grad(j, 1 - y, drecv[js, :].astype(F32))
        for cs in CHUNKS:
            total = dot_nt(dg[FULL:, :], wg[cs, :]) + dot_nt(du[FULL:, :], wu[cs, :])
            bsend[:, cs] = total.astype(BF16)

    def own_gradient():
        need("wg", "wu")
        for cs in CHUNKS:
            bown[:, cs] = dot_nt(dg[0:FULL, :], wg[cs, :]) + dot_nt(du[0:FULL, :], wu[cs, :])

    def hidden(block):
        need("wg", "wu")
        gate = dot(block, wg[...])
        up = dot(block, wu[...])
        return (gate * jax.nn.sigmoid(gate) * up).astype(BF16)

    def own_hidden():
        hown[...] = hidden(frow[0:FULL, :])

    def other_hidden(k):
        hsend[span(2 * k, 2), :] = hidden(frow[span(2 * k, 2, FULL), :])

    def forward_partial(k):
        need("wd")
        ks = span(2 * k, 2)
        for cs in CHUNKS:
            total = dot(hown[ks, :], wd[:, cs]) + dot(hrecv[ks, :], wdo[:, cs])
            fown[span(k), cs] = total[0:CAP, :]
            zsf[span(k), cs] = total[CAP:, :].astype(BF16)

    def forward_sum(k):
        total = (fown[span(k), :] + zrf[span(k), :].astype(F32)).astype(BF16)
        out = zdf if k else retf
        out[span(k), :] = total

    def gradient_partial(k):
        js = span(place(4 + k))
        zsb[span(k), :] = (bown[js, :] + brecv[js, :].astype(F32)).astype(BF16)

    def gradient_sum(k):
        js = span(place(k))
        total = bown[js, :] + brecv[js, :].astype(F32) + zrb[span(k), :].astype(F32)
        out = zdb if k else retb
        out[span(k), :] = total.astype(BF16)

    def forward_out():
        for cs in CHUNKS:
            fout[:, cs] = (xf[:, cs].astype(F32) + dot(f_hot[...], retf[:, cs])).astype(BF16)

    def gradient_out():
        need("xb")
        wide_b = xb[...].astype(F32)
        scale_b = lax.rsqrt(jnp.mean(wide_b * wide_b, axis=-1, keepdims=True) + EPS)
        gain_wide = gain[...].astype(F32)
        inner = jnp.zeros((TOK, 1), F32)
        for cs in CHUNKS:
            d_unit = dot(b_hot[...], retb[:, cs]) * gain_wide[:, cs]
            dn[:, cs] = d_unit
            inner = inner + jnp.sum(d_unit * (xb[:, cs].astype(F32) * scale_b), axis=-1, keepdims=True)
        inner = inner * (1.0 / D)
        for cs in CHUNKS:
            unit = xb[:, cs].astype(F32) * scale_b
            gout[:, cs] = (ct[:, cs].astype(F32) + scale_b * (dn[:, cs] - unit * inner)).astype(BF16)

    compute("prepC", cotangent_blocks)
    compute("prepF", forward_blocks)
    compute("dhown", own_d_hidden)
    compute("dhoth", other_d_hidden)
    compute("actown", own_activation)
    compute("bs", other_gradient)
    compute("bown", own_gradient)
    compute("hown", own_hidden)
    compute("cf", forward_out)
    compute("cb", gradient_out)
    for k in range(4):
        compute(f"h{k}", other_hidden, k)
        compute(f"fo{k}", forward_partial, k)
        compute(f"fa{k}", forward_sum, k)
        compute(f"ba{k}", gradient_partial, k)
        compute(f"bb{k}", gradient_sum, k)

    sent = []
    for step in ORDER:
        kind, name = step[0], step[1:]
        if kind == "~":
            function, given = computed[name]
            function(*given)
        elif name == "RF":
            if kind == "+":
                pl.when(p < 15)(copies[name].start)
            else:
                pl.when(p > 0)(copies[name].wait_recv)
        elif name == "RB":
            if kind == "+":
                pl.when(p > 0)(copies[name].start)
            else:
                pl.when(p < 15)(copies[name].wait_recv)
        elif kind == "+":
            copies[name].start()
            sent.append(name)
        else:
            copies[name].wait_recv()

    @pl.when(p == 0)
    def _():
        gout[...] = jnp.zeros_like(gout)
        zero = pltpu.make_async_copy(gout, nxt, ld.at[8])
        zero.start()
        zero.wait()

    @pl.when(p == 15)
    def _():
        fout[...] = jnp.zeros_like(fout)
        zero = pltpu.make_async_copy(fout, prv, ld.at[9])
        zero.start()
        zero.wait()

    for name in sent:
        copies[name].wait_send()
    pl.when(p < 15)(copies["RF"].wait_send)
    pl.when(p > 0)(copies["RB"].wait_send)


def hand_over(first, second, first_out, second_out, held, in_sem, out_sem):
    cut = TOK // 2
    steps = []
    for i, (src, dst) in enumerate(((first, first_out), (second, second_out))):
        for j in range(2):
            here = pl.ds(j * cut, cut)
            steps.append(
                (
                    pltpu.make_async_copy(src.at[here, :], held.at[i, here, :], in_sem.at[i, j]),
                    pltpu.make_async_copy(held.at[i, here, :], dst.at[here, :], out_sem.at[i, j]),
                )
            )
    for arrive, _ in steps:
        arrive.start()
    for arrive, leave in steps:
        arrive.wait()
        leave.start()
    for _, leave in steps:
        leave.wait()


def body(
    fwd_rows,
    fwd_experts,
    fwd_weight,
    back_rows,
    back_experts,
    back_weight,
    back_cotangent,
    norm_gain,
    w_gate,
    w_up,
    w_down,
    saved_gate,
    saved_up,
):
    vmem = pl.BlockSpec(memory_space=pltpu.VMEM)
    hbm = pl.BlockSpec(memory_space=pl.ANY)
    dma = pltpu.SemaphoreType.DMA
    out_shape = (jax.ShapeDtypeStruct((TOK, D), BF16), jax.ShapeDtypeStruct((TOK, D), BF16))

    def wide(count, kind=BF16):
        return pltpu.VMEM((count, D), kind)

    def narrow(count, kind=BF16):
        return pltpu.VMEM((count, FF), kind)

    outs = pl.pallas_call(
        kernel,
        out_shape=out_shape,
        in_specs=[vmem] * 5 + [hbm] * 8,
        out_specs=(hbm, hbm),
        scratch_shapes=[
            wide(TOK), wide(TOK), wide(TOK),
            narrow(D), narrow(D), wide(FF), wide(FF), narrow(512), narrow(512),
            wide(HALF), wide(HALF), wide(FULL), wide(2 * FULL),
            narrow(FULL, F32), narrow(FULL), narrow(FULL), narrow(512), narrow(512),
            wide(FULL), wide(FULL), wide(FULL, F32), wide(HALF), wide(HALF), wide(HALF), wide(HALF),
            narrow(FULL), narrow(FULL), narrow(FULL), wide(HALF, F32), wide(HALF), wide(HALF), wide(HALF),
            wide(HALF),
            wide(TOK), wide(TOK), wide(TOK, F32),
            pltpu.VMEM((TOK, HALF), BF16), pltpu.VMEM((TOK, HALF), BF16),
            dma((10,)), dma((W_PARTS,)), dma((W_PARTS,)), dma((8,)), dma((8,)), dma((8,)), dma((8,)),
            dma((8,)), dma((8,)), dma((1,)), dma((1,)), dma((8,)), dma((8,)),
            dma((4,)), dma((4,)), dma((4,)), dma((4,)), dma((4,)), dma((4,)),
            dma((4,)), dma((4,)), dma((4,)), dma((4,)), dma((2,)), dma((2,)),
        ],
        compiler_params=pltpu.CompilerParams(
            collective_id=0, has_side_effects=True, vmem_limit_bytes=56 * 2**20
        ),
        cost_estimate=pl.CostEstimate(flops=5_700_000_000, bytes_accessed=10_000_000, transcendentals=400_000),
    )(
        fwd_experts[0].T,
        fwd_weight[0].T,
        back_experts[0].T,
        back_weight[0].T,
        norm_gain,
        fwd_rows[0],
        back_rows[0],
        back_cotangent[0],
        w_gate[0, 0],
        w_up[0, 0],
        w_down[0, 0],
        saved_gate[0, 0],
        saved_up[0, 0],
    )
    outs = pl.pallas_call(
        hand_over,
        out_shape=out_shape,
        in_specs=[hbm, hbm],
        out_specs=(hbm, hbm),
        scratch_shapes=[pltpu.VMEM((2, TOK, D), BF16), dma((2, 2)), dma((2, 2))],
        compiler_params=pltpu.CompilerParams(vmem_limit_bytes=56 * 2**20),
    )(*outs)
    return outs[0][None], outs[1][None]


def solution(mesh):
    rows3 = P("pipe", "expert", None)
    rows4 = P("pipe", "expert", None, None)
    placed = (rows3,) * 7 + (P("pipe", None),) + (rows4,) * 5
    return jax.shard_map(
        body,
        mesh=mesh,
        in_specs=placed,
        out_specs=(rows3, rows3),
        check_vma=False,
    )
```

time: 188 us -> 159 us (0.85)
  the two profiles are of different devices: /device:TPU:37 before, /device:TPU:53 now
where the time goes in v2:
time: 159 us
  Pallas kernels  158 us (99%)
    pallas_call x1, Pallas kernels, body(): pl.pallas_call(kernel, out_shape=out_shape, in_specs=[vmem] * 5 + [hbm] *...  156 us

profile of v2, /device:TPU:53, one launch (start us, length us, event | category | flops | bytes accessed | tf_op | source)
XLA Modules:
  0.0 158.8 jit_solution(13149020891322588791)
XLA Ops:
  0.6 156.1 %shard_map.140 = (bf16[64,3584]{1,0:T(8,128)(2,1)}, bf16[64,3584]{1,0:T(8,128)(2,1)}) custom-call(s32[2,64]{1,0:T(2,128)} %bitcast.32, bf16[2,64]{1,0:T(2,128)(2,1)} %bitcast.34, s32[2,64]{1,0:T(2,128)} %bitcast.33, bf16[2,64]{1,0:T(2,128)(2,1)} %bitcast.35, bf16[1,3584]{1,0:T(2,128)(2,1)} %gain.1, bf16[64,3584]{1,0:T(8,128)(2,1)} %bitcast.25, ...), custom_call_target="tpu_custom_call" | custom-call | flops 5699999744 | bytes 10000000 | tf_op jit(solution)/shard_map/pallas_call | solution.py:410
  156.7 2.0 %shard_map.141 = (bf16[64,3584]{1,0:T(8,128)(2,1)}, bf16[64,3584]{1,0:T(8,128)(2,1)}) custom-call(bf16[64,3584]{1,0:T(8,128)(2,1)} %get-tuple-element.6.first, bf16[64,3584]{1,0:T(8,128)(2,1)} %get-tuple-element.7.second), custom_call_target="tpu_custom_call" | custom-call | tf_op jit(solution)/shard_map/pallas_call | solution.py:449

commit v3 on v2

--- a/solution.py
+++ b/solution.py
@@ -15,23 +15,25 @@
 COLS = 512
 CHUNKS = [slice(c, c + COLS) for c in range(0, D, COLS)]
 W_PARTS = 8
+Y_BY_Z = ()
+G_BY_Z = (0,)
 EPS = 1e-06
 F32 = jnp.float32
 BF16 = jnp.bfloat16
 
 ORDER = [
-    "~prepC", "+C4", "+C1", "+W0", "+W1", "+W2", "+W3", "~prepF", "+F2", "+F3", "+W4", "+W5", "?C1",
-    "+W6", "+F4", "+W7", "?F3", "+Y3", "?F2", "+F6", "+F7", "+C2", "+F1", "?W0", "?F1", "+F5",
-    "?F6", "+Y6", "+C3", "?W1", "?W2", "?F7", "?W3", "?C2", "+Y2", "+C6", "?W4", "?F4", "+Y7",
-    "+C5", "?W5", "?W6", "?Y6", "?C3", "+C7", "?F5", "?Y3", "?Y2", "~h2", "+H2", "+Y1", "?C5",
-    "?Y7", "~h3", "+H3", "~hown", "?W7", "+Y5", "?H2", "~fo2", "+FP2", "?C6", "?H3", "~fo3", "+FP3",
-    "+Y0", "?FP2", "~fa2", "+FD2", "?C7", "?C4", "?Y1", "?Y5", "~h1", "+H1", "~dhoth", "+D", "?FP3",
-    "~fa3", "+FD3", "+Y4", "?H1", "~fo1", "?Y0", "+FP1", "?D", "~bs", "+G7", "~dhown", "~actown",
-    "?Y4", "~h0", "+H0", "+G5", "+G3", "~bown", "+G6", "?G7", "~ba3", "+G4", "+BP3", "?FD2", "?H0",
-    "~fo0", "+FP0", "?G5", "~ba1", "?FP1", "?BP3", "+BP1", "~fa1", "?G3", "+FD1", "?FP0", "+G1",
-    "~bb3", "+BD3", "?G6", "?FD3", "~ba2", "+G2", "+BP2", "?G4", "?BP1", "~ba0", "+BP0", "?G1",
-    "~bb1", "+G0", "+BD1", "?G2", "?BP2", "~bb2", "+BD2", "?BD3", "?FD1", "?BP0", "~fa0", "~cf",
-    "+RF", "?G0", "~bb0", "?BD1", "?BD2", "~cb", "+RB", "?RF", "?RB"
+    "~prepC", "+W0", "+C4", "+W1", "+W2", "+W3", "+W4", "+C1", "~prepF", "+F3", "+F4", "+W5", "+F2",
+    "+W6", "+F1", "+W7", "+C2", "?C1", "+C3", "?F3", "+F7", "+C5", "?W0", "?W1", "?F1", "?W2",
+    "?F2", "?W3", "+Y3", "+Y2", "?F7", "+Y7", "?C2", "+C6", "?W4", "?C3", "+C7", "?Y3", "?F4",
+    "?C4", "?W5", "?W6", "+F6", "?C7", "?C5", "+F5", "?W7", "?C6", "~dhown", "~actown", "~dhoth",
+    "+D", "?Y7", "?F6", "+Y6", "~bown", "~ba0", "+BP0", "?D", "~h3", "+H3", "~bs", "+G4", "+G7",
+    "?H3", "?Y6", "?Y2", "?F5", "+G5", "~hown", "~fo3", "~h2", "+FP3", "+H2", "+Y1", "?G7", "~ba3",
+    "+BP3", "+Y5", "?H2", "+G3", "?FP3", "~fa3", "~fo2", "+FP2", "?G5", "+FD3", "?Y1", "~ba1",
+    "+BP1", "?Y5", "~h1", "+H1", "+Y0", "?H1", "?FP2", "+Y4", "?BP3", "+G6", "?G3", "~bb3", "+BD3",
+    "~fo1", "?G4", "+FP1", "?BP0", "~fa2", "+FD2", "?FD3", "?Y0", "~gs0", "?Y4", "~h0", "+H0",
+    "+G1", "?H0", "?FP1", "~fa1", "?G6", "~ba2", "+G2", "+FD1", "+BP2", "?FD2", "?BP1", "~fo0",
+    "+FP0", "?G1", "?BD3", "~bb1", "+BD1", "?BP2", "?FD1", "+G0", "?G2", "~bb2", "+BD2", "?FP0",
+    "~fa0", "~cf", "+RF", "?G0", "~bb0", "?BD1", "?BD2", "~cb", "+RB", "?RB", "?RF"
 ]
 
 
@@ -84,7 +86,7 @@
     xf, xb, ct, wg, wu, wd, wdo, sg, su,
     csend, fsend, crow, frow,
     dho, dsend, drecv, dg, du,
-    bsend, brecv, bown, zsb, zrb, zdb, retb,
+    bsend, brecv, gadd, bown, zsb, zrb, zdb, retb,
     hown, hsend, hrecv, fown, zsf, zrf, zdf, retf,
     fout, gout, dn, b_hot, f_hot,
     ld, s_w, r_w, s_c, r_c, s_f, r_f, s_y, r_y, s_d, r_d, s_g, r_g,
@@ -170,8 +172,16 @@
                 s_sem.at[4 + k], r_sem.at[4 + k], z_partner,
             )
     for j in range(8):
-        remote(f"Y{j}", rows(frow, place(j)), rows(frow, 8 + place(j)), s_y.at[j], r_y.at[j], y_partner)
-        remote(f"G{j}", rows(bsend, place(j)), rows(brecv, place(j)), s_g.at[j], r_g.at[j], y_partner)
+        if j - 4 in Y_BY_Z:
+            remote(
+                f"Y{j}", rows(frow, 8 + place(j - 4)), rows(frow, 8 + place(j)), s_y.at[j], r_y.at[j], z_partner
+            )
+        else:
+            remote(f"Y{j}", rows(frow, place(j)), rows(frow, 8 + place(j)), s_y.at[j], r_y.at[j], y_partner)
+        if j - 4 in G_BY_Z:
+            remote(f"G{j}", rows(bsend, place(j)), rows(gadd, j - 4), s_g.at[j], r_g.at[j], z_partner)
+        else:
+            remote(f"G{j}", rows(bsend, place(j)), rows(brecv, place(j)), s_g.at[j], r_g.at[j], y_partner)
     remote("D", dsend, drecv, s_d.at[0], r_d.at[0], y_partner)
     for k in range(4):
         remote(f"H{k}", rows(hsend, 2 * k, 2), rows(hrecv, 2 * k, 2), s_h.at[k], r_h.at[k], y_partner)
@@ -272,9 +282,16 @@
         out = zdf if k else retf
         out[span(k), :] = total
 
+    def gradient_across(k):
+        js = span(place(k))
+        bsend[js, :] = (bsend[js, :].astype(F32) + gadd[span(k), :].astype(F32)).astype(BF16)
+
     def gradient_partial(k):
         js = span(place(4 + k))
-        zsb[span(k), :] = (bown[js, :] + brecv[js, :].astype(F32)).astype(BF16)
+        total = bown[js, :]
+        if k not in G_BY_Z:
+            total = total + brecv[js, :].astype(F32)
+        zsb[span(k), :] = total.astype(BF16)
 
     def gradient_sum(k):
         js = span(place(k))
@@ -315,6 +332,7 @@
         compute(f"h{k}", other_hidden, k)
         compute(f"fo{k}", forward_partial, k)
         compute(f"fa{k}", forward_sum, k)
+        compute(f"gs{k}", gradient_across, k)
         compute(f"ba{k}", gradient_partial, k)
         compute(f"bb{k}", gradient_sum, k)
 
@@ -417,7 +435,7 @@
             narrow(D), narrow(D), wide(FF), wide(FF), narrow(512), narrow(512),
             wide(HALF), wide(HALF), wide(FULL), wide(2 * FULL),
             narrow(FULL, F32), narrow(FULL), narrow(FULL), narrow(512), narrow(512),
-            wide(FULL), wide(FULL), wide(FULL, F32), wide(HALF), wide(HALF), wide(HALF), wide(HALF),
+            wide(FULL), wide(FULL), wide(HALF), wide(FULL, F32), wide(HALF), wide(HALF), wide(HALF), wide(HALF),
             narrow(FULL), narrow(FULL), narrow(FULL), wide(HALF, F32), wide(HALF), wide(HALF), wide(HALF),
             wide(HALF),
             wide(TOK), wide(TOK), wide(TOK, F32),

time: 159 us -> 150 us (0.943)
  the two profiles are of different devices: /device:TPU:53 before, /device:TPU:37 now
where the time goes in v3:
time: 150 us; the launch traced here: 148 us
  Pallas kernels  147 us (98%)
    pallas_call x1, Pallas kernels, body(): pl.pallas_call(kernel, out_shape=out_shape, in_specs=[vmem] * 5 + [hbm] *...  145 us

profile of v3, /device:TPU:37, one launch (start us, length us, event | category | flops | bytes accessed | tf_op | source)
XLA Modules:
  0.0 147.7 jit_solution(6497996224819926973)
XLA Ops:
  0.6 145.0 %shard_map.140 = (bf16[64,3584]{1,0:T(8,128)(2,1)}, bf16[64,3584]{1,0:T(8,128)(2,1)}) custom-call(s32[2,64]{1,0:T(2,128)} %bitcast.32, bf16[2,64]{1,0:T(2,128)(2,1)} %bitcast.34, s32[2,64]{1,0:T(2,128)} %bitcast.33, bf16[2,64]{1,0:T(2,128)(2,1)} %bitcast.35, bf16[1,3584]{1,0:T(2,128)(2,1)} %gain.1, bf16[64,3584]{1,0:T(8,128)(2,1)} %bitcast.25, ...), custom_call_target="tpu_custom_call" | custom-call | flops 5699999744 | bytes 10000000 | tf_op jit(solution)/shard_map/pallas_call | solution.py:428
  145.6 2.0 %shard_map.141 = (bf16[64,3584]{1,0:T(8,128)(2,1)}, bf16[64,3584]{1,0:T(8,128)(2,1)}) custom-call(bf16[64,3584]{1,0:T(8,128)(2,1)} %get-tuple-element.6.first, bf16[64,3584]{1,0:T(8,128)(2,1)} %get-tuple-element.7.second), custom_call_target="tpu_custom_call" | custom-call | tf_op jit(solution)/shard_map/pallas_call | solution.py:467

commit v4 on v3

--- a/solution.py
+++ b/solution.py
@@ -16,24 +16,24 @@
 CHUNKS = [slice(c, c + COLS) for c in range(0, D, COLS)]
 W_PARTS = 8
 Y_BY_Z = ()
-G_BY_Z = (0,)
+G_BY_Z = (1,)
 EPS = 1e-06
 F32 = jnp.float32
 BF16 = jnp.bfloat16
 
 ORDER = [
-    "~prepC", "+W0", "+C4", "+W1", "+W2", "+W3", "+W4", "+C1", "~prepF", "+F3", "+F4", "+W5", "+F2",
-    "+W6", "+F1", "+W7", "+C2", "?C1", "+C3", "?F3", "+F7", "+C5", "?W0", "?W1", "?F1", "?W2",
-    "?F2", "?W3", "+Y3", "+Y2", "?F7", "+Y7", "?C2", "+C6", "?W4", "?C3", "+C7", "?Y3", "?F4",
-    "?C4", "?W5", "?W6", "+F6", "?C7", "?C5", "+F5", "?W7", "?C6", "~dhown", "~actown", "~dhoth",
-    "+D", "?Y7", "?F6", "+Y6", "~bown", "~ba0", "+BP0", "?D", "~h3", "+H3", "~bs", "+G4", "+G7",
-    "?H3", "?Y6", "?Y2", "?F5", "+G5", "~hown", "~fo3", "~h2", "+FP3", "+H2", "+Y1", "?G7", "~ba3",
-    "+BP3", "+Y5", "?H2", "+G3", "?FP3", "~fa3", "~fo2", "+FP2", "?G5", "+FD3", "?Y1", "~ba1",
-    "+BP1", "?Y5", "~h1", "+H1", "+Y0", "?H1", "?FP2", "+Y4", "?BP3", "+G6", "?G3", "~bb3", "+BD3",
-    "~fo1", "?G4", "+FP1", "?BP0", "~fa2", "+FD2", "?FD3", "?Y0", "~gs0", "?Y4", "~h0", "+H0",
-    "+G1", "?H0", "?FP1", "~fa1", "?G6", "~ba2", "+G2", "+FD1", "+BP2", "?FD2", "?BP1", "~fo0",
-    "+FP0", "?G1", "?BD3", "~bb1", "+BD1", "?BP2", "?FD1", "+G0", "?G2", "~bb2", "+BD2", "?FP0",
-    "~fa0", "~cf", "+RF", "?G0", "~bb0", "?BD1", "?BD2", "~cb", "+RB", "?RB", "?RF"
+    "~enter", "+F3", "+W0", "+W1", "+F4", "+C4", "+W2", "+W3", "+W4", "+C2", "+W5", "+W6", "?W0",
+    "+F1", "?F3", "+F7", "+F2", "?W1", "+C3", "+Y3", "?F1", "+F5", "?W2", "?C2", "?F7", "+Y7",
+    "+C6", "?F2", "+W7", "+F6", "?C3", "?Y3", "+C1", "+C7", "?F4", "?F5", "+Y1", "?Y7", "~h3",
+    "+H3", "?W3", "?C1", "+C5", "?F6", "?W4", "~hown", "+Y5", "?Y1", "?W5", "?W6", "?C4", "?H3",
+    "?W7", "~fo3", "+FP3", "?C6", "+Y2", "?C5", "?C7", "~dhown", "~actown", "~bown", "~ba1", "+BP1",
+    "?Y5", "~h1", "+H1", "+Y6", "?FP3", "~fa3", "+FD3", "?Y2", "~dhoth", "?H1", "+D", "~fo1",
+    "+FP1", "?Y6", "+Y4", "~h2", "?D", "~bs", "+H2", "+G5", "+G7", "+Y0", "?H2", "~fo2", "+FP2",
+    "?G7", "~ba3", "+BP3", "?FP1", "~fa1", "+G6", "?BP1", "+FD1", "?Y4", "?Y0", "~h0", "+H0", "+G3",
+    "?FP2", "~fa2", "+FD2", "?G6", "~ba2", "?H0", "+BP2", "+G2", "?BP3", "+G4", "?G5", "?G3",
+    "~bb3", "+BD3", "~fo0", "+FP0", "?G2", "~gs1", "+G1", "?BP2", "~bb2", "+BD2", "?G4", "~ba0",
+    "+G0", "+BP0", "?FD3", "?FP0", "?FD2", "?BD3", "~fa0", "?FD1", "~cf", "?G1", "~bb1", "+BD1",
+    "+RF", "?BP0", "?G0", "~bb0", "?BD1", "?BD2", "~cb", "+RB", "?RF", "?RB"
 ]
 
 
@@ -206,7 +206,6 @@
         for cs in CHUNKS:
             csend[:, cs] = dot(gather, ct[:, cs]).astype(BF16)
         crow[span(0), :] = csend[span(0), :]
-        pl.semaphore_wait(barrier, len(friends))
 
     def forward_blocks():
         masks = selection(fids[...], slot_experts)
@@ -219,6 +218,9 @@
         for cs in CHUNKS:
             fsend[:, cs] = dot(gather, fout[:, cs]).astype(BF16)
         frow[span(0), :] = fsend[span(0), :]
+
+    def enter():
+        pl.semaphore_wait(barrier, len(friends))
 
     def own_d_hidden():
         need("wd")
@@ -318,8 +320,7 @@
             unit = xb[:, cs].astype(F32) * scale_b
             gout[:, cs] = (ct[:, cs].astype(F32) + scale_b * (dn[:, cs] - unit * inner)).astype(BF16)
 
-    compute("prepC", cotangent_blocks)
-    compute("prepF", forward_blocks)
+    compute("enter", enter)
     compute("dhown", own_d_hidden)
     compute("dhoth", other_d_hidden)
     compute("actown", own_activation)
@@ -336,6 +337,8 @@
         compute(f"ba{k}", gradient_partial, k)
         compute(f"bb{k}", gradient_sum, k)
 
+    cotangent_blocks()
+    forward_blocks()
     sent = []
     for step in ORDER:
         kind, name = step[0], step[1:]

time: 150 us -> 148 us (0.987)
  Pallas kernels: 147 us -> 144 us
    pallas_call x1, Pallas kernels: 145 us -> 142 us  [body(): pl.pallas_call(kernel, out_shape=out_shape, in_specs=[vmem] * 5 + [hbm] *...]
where the time goes in v4:
time: 148 us; the launch traced here: 145 us
  Pallas kernels  144 us (97%)
    pallas_call x1, Pallas kernels, body(): pl.pallas_call(kernel, out_shape=out_shape, in_specs=[vmem] * 5 + [hbm] *...  142 us

profile of v4, /device:TPU:37, one launch (start us, length us, event | category | flops | bytes accessed | tf_op | source)
XLA Modules:
  0.0 145.1 jit_solution(6876659940810045239)
XLA Ops:
  0.6 142.4 %shard_map.140 = (bf16[64,3584]{1,0:T(8,128)(2,1)}, bf16[64,3584]{1,0:T(8,128)(2,1)}) custom-call(s32[2,64]{1,0:T(2,128)} %bitcast.32, bf16[2,64]{1,0:T(2,128)(2,1)} %bitcast.34, s32[2,64]{1,0:T(2,128)} %bitcast.33, bf16[2,64]{1,0:T(2,128)(2,1)} %bitcast.35, bf16[1,3584]{1,0:T(2,128)(2,1)} %gain.1, bf16[64,3584]{1,0:T(8,128)(2,1)} %bitcast.25, ...), custom_call_target="tpu_custom_call" | custom-call | flops 5699999744 | bytes 10000000 | tf_op jit(solution)/shard_map/pallas_call | solution.py:431
  143.0 2.0 %shard_map.141 = (bf16[64,3584]{1,0:T(8,128)(2,1)}, bf16[64,3584]{1,0:T(8,128)(2,1)}) custom-call(bf16[64,3584]{1,0:T(8,128)(2,1)} %get-tuple-element.6.first, bf16[64,3584]{1,0:T(8,128)(2,1)} %get-tuple-element.7.second), custom_call_target="tpu_custom_call" | custom-call | tf_op jit(solution)/shard_map/pallas_call | solution.py:470

commit v5 on v4

--- a/solution.py
+++ b/solution.py
@@ -16,24 +16,24 @@
 CHUNKS = [slice(c, c + COLS) for c in range(0, D, COLS)]
 W_PARTS = 8
 Y_BY_Z = ()
-G_BY_Z = (1,)
+G_BY_Z = (0,)
 EPS = 1e-06
 F32 = jnp.float32
 BF16 = jnp.bfloat16
 
 ORDER = [
-    "~enter", "+F3", "+W0", "+W1", "+F4", "+C4", "+W2", "+W3", "+W4", "+C2", "+W5", "+W6", "?W0",
-    "+F1", "?F3", "+F7", "+F2", "?W1", "+C3", "+Y3", "?F1", "+F5", "?W2", "?C2", "?F7", "+Y7",
-    "+C6", "?F2", "+W7", "+F6", "?C3", "?Y3", "+C1", "+C7", "?F4", "?F5", "+Y1", "?Y7", "~h3",
-    "+H3", "?W3", "?C1", "+C5", "?F6", "?W4", "~hown", "+Y5", "?Y1", "?W5", "?W6", "?C4", "?H3",
-    "?W7", "~fo3", "+FP3", "?C6", "+Y2", "?C5", "?C7", "~dhown", "~actown", "~bown", "~ba1", "+BP1",
-    "?Y5", "~h1", "+H1", "+Y6", "?FP3", "~fa3", "+FD3", "?Y2", "~dhoth", "?H1", "+D", "~fo1",
-    "+FP1", "?Y6", "+Y4", "~h2", "?D", "~bs", "+H2", "+G5", "+G7", "+Y0", "?H2", "~fo2", "+FP2",
-    "?G7", "~ba3", "+BP3", "?FP1", "~fa1", "+G6", "?BP1", "+FD1", "?Y4", "?Y0", "~h0", "+H0", "+G3",
-    "?FP2", "~fa2", "+FD2", "?G6", "~ba2", "?H0", "+BP2", "+G2", "?BP3", "+G4", "?G5", "?G3",
-    "~bb3", "+BD3", "~fo0", "+FP0", "?G2", "~gs1", "+G1", "?BP2", "~bb2", "+BD2", "?G4", "~ba0",
-    "+G0", "+BP0", "?FD3", "?FP0", "?FD2", "?BD3", "~fa0", "?FD1", "~cf", "?G1", "~bb1", "+BD1",
-    "+RF", "?BP0", "?G0", "~bb0", "?BD1", "?BD2", "~cb", "+RB", "?RF", "?RB"
+    "~enter", "+C2", "+F1", "+F3", "+C1", "+W0", "+C4", "+W1", "+W2", "?C2", "+W3", "+C6", "?W0",
+    "?F1", "+F5", "+W4", "+W5", "+C3", "?C6", "?F3", "+Y3", "+F7", "+W6", "?F5", "?W1", "?W2",
+    "?C1", "+F2", "?W3", "+C5", "?W4", "+Y5", "?C3", "?W5", "?Y3", "+C7", "?F7", "?C4", "+Y1",
+    "+W7", "+Y7", "+F4", "?F2", "+F6", "?C7", "?C5", "~dhown", "~actown", "?Y1", "~bown", "?Y5",
+    "~ba0", "?W6", "~h1", "+H1", "?W7", "+BP0", "~dhoth", "+D", "?F4", "?F6", "~hown", "?Y7", "~h3",
+    "+H3", "+Y2", "?H1", "~fo1", "+FP1", "?D", "~bs", "+G7", "+Y6", "?H3", "~fo3", "+FP3", "+G4",
+    "?FP3", "?G7", "+G3", "~fa3", "+FD3", "~ba3", "+BP3", "?Y2", "?Y6", "~h2", "?FP1", "~fa1",
+    "+H2", "+G5", "+G6", "?H2", "~fo2", "+Y0", "+FP2", "?G5", "~ba1", "?BP3", "+FD1", "+BP1", "+Y4",
+    "?G6", "+G1", "?FP2", "~fa2", "~ba2", "+FD2", "?G3", "~bb3", "+BD3", "?G4", "?FD3", "+BP2",
+    "?Y0", "?Y4", "~h0", "+H0", "+G2", "?H0", "?G1", "?FD2", "?BP1", "~gs0", "~bb1", "+G0", "+BD1",
+    "~fo0", "+FP0", "?G2", "?BP2", "~bb2", "?FD1", "+BD2", "?BP0", "?FP0", "~fa0", "~cf", "+RF",
+    "?G0", "~bb0", "?BD2", "?BD1", "?BD3", "~cb", "+RB", "?RB", "?RF"
 ]
 
 

time: 148 us -> 146 us (0.986); the launches traced: 145 us -> 146 us
  no operation moved by 1% of the time
where the time goes in v5:
time: 146 us
  Pallas kernels  145 us (99%)
    pallas_call x1, Pallas kernels, body(): pl.pallas_call(kernel, out_shape=out_shape, in_specs=[vmem] * 5 + [hbm] *...  143 us

profile of v5, /device:TPU:37, one launch (start us, length us, event | category | flops | bytes accessed | tf_op | source)
XLA Modules:
  0.0 146.0 jit_solution(3899822259866813113)
XLA Ops:
  0.6 143.3 %shard_map.140 = (bf16[64,3584]{1,0:T(8,128)(2,1)}, bf16[64,3584]{1,0:T(8,128)(2,1)}) custom-call(s32[2,64]{1,0:T(2,128)} %bitcast.32, bf16[2,64]{1,0:T(2,128)(2,1)} %bitcast.34, s32[2,64]{1,0:T(2,128)} %bitcast.33, bf16[2,64]{1,0:T(2,128)(2,1)} %bitcast.35, bf16[1,3584]{1,0:T(2,128)(2,1)} %gain.1, bf16[64,3584]{1,0:T(8,128)(2,1)} %bitcast.25, ...), custom_call_target="tpu_custom_call" | custom-call | flops 5699999744 | bytes 10000000 | tf_op jit(solution)/shard_map/pallas_call | solution.py:431
  144.0 2.0 %shard_map.141 = (bf16[64,3584]{1,0:T(8,128)(2,1)}, bf16[64,3584]{1,0:T(8,128)(2,1)}) custom-call(bf16[64,3584]{1,0:T(8,128)(2,1)} %get-tuple-element.6.first, bf16[64,3584]{1,0:T(8,128)(2,1)} %get-tuple-element.7.second), custom_call_target="tpu_custom_call" | custom-call | tf_op jit(solution)/shard_map/pallas_call | solution.py:470

commit v6 on v5

--- a/solution.py
+++ b/solution.py
@@ -190,8 +190,9 @@
     for k in (1, 2, 3):
         remote(f"BD{k}", rows(zdb, k), rows(retb, k), s_bd.at[k], r_bd.at[k], dev(sources[k]))
         remote(f"FD{k}", rows(zdf, k), rows(retf, k), s_fd.at[k], r_fd.at[k], dev(sources[k]))
-    remote("RF", fout, nxt, s_out.at[0], r_out.at[0], later)
-    remote("RB", gout, prv, s_out.at[1], r_out.at[1], earlier)
+    for h in range(2):
+        remote(f"RF{h}", rows(fout, h), rows(nxt, h), s_out.at[h], r_out.at[h], later)
+        remote(f"RB{h}", rows(gout, h), rows(prv, h), s_out.at[2 + h], r_out.at[2 + h], earlier)
 
     computed = {}
 
@@ -301,24 +302,26 @@
         out = zdb if k else retb
         out[span(k), :] = total.astype(BF16)
 
-    def forward_out():
-        for cs in CHUNKS:
-            fout[:, cs] = (xf[:, cs].astype(F32) + dot(f_hot[...], retf[:, cs])).astype(BF16)
-
-    def gradient_out():
+    def forward_out(h):
+        hs = span(h)
+        for cs in CHUNKS:
+            fout[hs, cs] = (xf[hs, cs].astype(F32) + dot(f_hot[hs, :], retf[:, cs])).astype(BF16)
+
+    def gradient_out(h):
         need("xb")
-        wide_b = xb[...].astype(F32)
+        hs = span(h)
+        wide_b = xb[hs, :].astype(F32)
         scale_b = lax.rsqrt(jnp.mean(wide_b * wide_b, axis=-1, keepdims=True) + EPS)
         gain_wide = gain[...].astype(F32)
-        inner = jnp.zeros((TOK, 1), F32)
-        for cs in CHUNKS:
-            d_unit = dot(b_hot[...], retb[:, cs]) * gain_wide[:, cs]
-            dn[:, cs] = d_unit
-            inner = inner + jnp.sum(d_unit * (xb[:, cs].astype(F32) * scale_b), axis=-1, keepdims=True)
+        inner = jnp.zeros((CAP, 1), F32)
+        for cs in CHUNKS:
+            d_unit = dot(b_hot[hs, :], retb[:, cs]) * gain_wide[:, cs]
+            dn[hs, cs] = d_unit
+            inner = inner + jnp.sum(d_unit * (xb[hs, cs].astype(F32) * scale_b), axis=-1, keepdims=True)
         inner = inner * (1.0 / D)
         for cs in CHUNKS:
-            unit = xb[:, cs].astype(F32) * scale_b
-            gout[:, cs] = (ct[:, cs].astype(F32) + scale_b * (dn[:, cs] - unit * inner)).astype(BF16)
+            unit = xb[hs, cs].astype(F32) * scale_b
+            gout[hs, cs] = (ct[hs, cs].astype(F32) + scale_b * (dn[hs, cs] - unit * inner)).astype(BF16)
 
     compute("enter", enter)
     compute("dhown", own_d_hidden)
@@ -327,8 +330,8 @@
     compute("bs", other_gradient)
     compute("bown", own_gradient)
     compute("hown", own_hidden)
-    compute("cf", forward_out)
-    compute("cb", gradient_out)
+    compute("cf", forward_out, 0)
+    compute("cb", gradient_out, 0)
     for k in range(4):
         compute(f"h{k}", other_hidden, k)
         compute(f"fo{k}", forward_partial, k)
@@ -347,14 +350,20 @@
             function(*given)
         elif name == "RF":
             if kind == "+":
-                pl.when(p < 15)(copies[name].start)
+                pl.when(p < 15)(copies["RF0"].start)
+                forward_out(1)
+                pl.when(p < 15)(copies["RF1"].start)
             else:
-                pl.when(p > 0)(copies[name].wait_recv)
+                for h in range(2):
+                    pl.when(p > 0)(copies[f"RF{h}"].wait_recv)
         elif name == "RB":
             if kind == "+":
-                pl.when(p > 0)(copies[name].start)
+                pl.when(p > 0)(copies["RB0"].start)
+                gradient_out(1)
+                pl.when(p > 0)(copies["RB1"].start)
             else:
-                pl.when(p < 15)(copies[name].wait_recv)
+                for h in range(2):
+                    pl.when(p < 15)(copies[f"RB{h}"].wait_recv)
         elif kind == "+":
             copies[name].start()
             sent.append(name)
@@ -377,8 +386,9 @@
 
     for name in sent:
         copies[name].wait_send()
-    pl.when(p < 15)(copies["RF"].wait_send)
-    pl.when(p > 0)(copies["RB"].wait_send)
+    for h in range(2):
+        pl.when(p < 15)(copies[f"RF{h}"].wait_send)
+        pl.when(p > 0)(copies[f"RB{h}"].wait_send)
 
 
 def hand_over(first, second, first_out, second_out, held, in_sem, out_sem):
@@ -446,7 +456,7 @@
             dma((10,)), dma((W_PARTS,)), dma((W_PARTS,)), dma((8,)), dma((8,)), dma((8,)), dma((8,)),
             dma((8,)), dma((8,)), dma((1,)), dma((1,)), dma((8,)), dma((8,)),
             dma((4,)), dma((4,)), dma((4,)), dma((4,)), dma((4,)), dma((4,)),
-            dma((4,)), dma((4,)), dma((4,)), dma((4,)), dma((2,)), dma((2,)),
+            dma((4,)), dma((4,)), dma((4,)), dma((4,)), dma((4,)), dma((4,)),
         ],
         compiler_params=pltpu.CompilerParams(
             collective_id=0, has_side_effects=True, vmem_limit_bytes=56 * 2**20

time: 146 us -> 146 us (level)
  no operation moved by 1% of the time
where the time goes in v6:
time: 146 us
  Pallas kernels  145 us (99%)
    pallas_call x1, Pallas kernels, body(): pl.pallas_call(kernel, out_shape=out_shape, in_specs=[vmem] * 5 + [hbm] *...  143 us

profile of v6, /device:TPU:37, one launch (start us, length us, event | category | flops | bytes accessed | tf_op | source)
XLA Modules:
  0.0 145.9 jit_solution(8939559841229854378)
XLA Ops:
  0.6 143.2 %shard_map.140 = (bf16[64,3584]{1,0:T(8,128)(2,1)}, bf16[64,3584]{1,0:T(8,128)(2,1)}) custom-call(s32[2,64]{1,0:T(2,128)} %bitcast.32, bf16[2,64]{1,0:T(2,128)(2,1)} %bitcast.34, s32[2,64]{1,0:T(2,128)} %bitcast.33, bf16[2,64]{1,0:T(2,128)(2,1)} %bitcast.35, bf16[1,3584]{1,0:T(2,128)(2,1)} %gain.1, bf16[64,3584]{1,0:T(8,128)(2,1)} %bitcast.25, ...), custom_call_target="tpu_custom_call" | custom-call | flops 5699999744 | bytes 10000000 | tf_op jit(solution)/shard_map/pallas_call | solution.py:441
  143.8 2.0 %shard_map.141 = (bf16[64,3584]{1,0:T(8,128)(2,1)}, bf16[64,3584]{1,0:T(8,128)(2,1)}) custom-call(bf16[64,3584]{1,0:T(8,128)(2,1)} %get-tuple-element.6.first, bf16[64,3584]{1,0:T(8,128)(2,1)} %get-tuple-element.7.second), custom_call_target="tpu_custom_call" | custom-call | tf_op jit(solution)/shard_map/pallas_call | solution.py:480
